TPU v7x, 512 devices: a whole 4x8x8 slice. The times are simulated.
512 devices in a mesh: cfg: 2 (over z_hi), batch: 32 (over z_lo, x, core), seq: 8 (over y).
Axes of the slice: x: 4, y: 8, z: 8 (z_hi: 2, z_lo: 4; z = z_hi * 4 + z_lo), core: 2. Of those that a mesh axis runs over, the one named last changes fastest.
Arguments:
- query_rows: bfloat16 [2, 40960, 4096], P('cfg', ('batch', 'seq')), parts along dimension 1, may hold values from -32 to 32
- key_rows: bfloat16 [2, 40960, 4096], P('cfg', ('batch', 'seq')), parts along dimension 1, may hold values from -32 to 32
- value_rows: bfloat16 [2, 40960, 4096], P('cfg', ('batch', 'seq')), parts along dimension 1, may hold values from -6 to 6
- query_gain: float32 [4096], replicated, may hold values from 0.25 to 1.75
- key_gain: float32 [4096], replicated, may hold values from 0.25 to 1.75
- out_map: bfloat16 [4096, 64], replicated, may hold values from -0.09375 to 0.09375
- latents: float32 [40960, 64], P(('batch', 'seq')), parts along dimension 0, may hold values from -6 to 6
- step_index: int32 [1], replicated, may hold values from 0 to 49
Outputs:
- next_latents: float32 [40960, 64], P(('batch', 'seq')), parts along dimension 0
- denoised: float32 [40960, 64], P(('batch', 'seq')), parts along dimension 0
There are 32 independent parts, one for each index of `batch`. A program takes and returns all parts, laid end to end along the dimension named above; an argument that names none is the same for every part. Nothing has to cross between parts.
All inputs are finite; a program needn't handle non-finite values.
Results may differ from a plain program's by a relative error of at most 0.0025.
The roundings to bfloat16 on the way count: a program that leaves them out, or rounds other values in their place, can miss the bound.
Values may be sent and summed in bfloat16 or wider, within the bound.
No kernel may reach another device: no remote copies, remote signals or barrier semaphores. Data moves between devices by JAX's collectives and lax.ppermute only.
A program may use at most 64 MiB of HBM per device.

v0:
```python
import math

import jax
import jax.numpy as jnp
from jax import lax
from jax.sharding import PartitionSpec as P

HEADS = 32
HEAD_DIM = 128
STEPS = 50


GUIDANCE = 5.0
FLOW_SHIFT = 5.0
EPSILON = 1e-06


def normalize(rows_in, gain_row):
    values = rows_in.astype(jnp.float32)
    mean_square = jnp.mean(values * values, axis=-1, keepdims=True)
    return (values * lax.rsqrt(mean_square + EPSILON) * gain_row).astype(jnp.bfloat16)


def sigma_at(progress):
    remain = 1.0 - progress / STEPS
    return FLOW_SHIFT * remain / (1.0 + (FLOW_SHIFT - 1.0) * remain)


def block_count(length):
    pieces = max(1, length // 512)
    while length % pieces:
        pieces -= 1
    return pieces


def attend(query_part, key_part, value_part):
    length, heads_here, head_width = query_part.shape
    pieces = block_count(length)
    block_rows = length // pieces
    score_scale = 1.0 / math.sqrt(head_width)

    def one_block(query_block):
        scores = (
            jnp.einsum("qhd,khd->hqk", query_block, key_part, preferred_element_type=jnp.float32)
            * score_scale
        )
        row_top = jnp.max(scores, axis=-1, keepdims=True)
        weights = jnp.exp(scores - row_top)
        weights_bf = (weights / jnp.sum(weights, axis=-1, keepdims=True)).astype(jnp.bfloat16)
        return jnp.einsum(
            "hqk,khd->qhd", weights_bf, value_part, preferred_element_type=jnp.float32
        ).astype(jnp.bfloat16)

    attended = lax.map(one_block, query_part.reshape(pieces, block_rows, heads_here, head_width))
    return attended.reshape(length, heads_here, head_width)


def attend_pair(members):
    row_count = members[0].shape[0]
    heads_here = members[0].shape[2]
    half_rows = row_count // 2
    flattened = [member.reshape(row_count, heads_here, HEAD_DIM) for member in members]
    leading = attend(flattened[0][:half_rows], flattened[1][:half_rows], flattened[2][:half_rows])
    trailing = attend(flattened[0][half_rows:], flattened[1][half_rows:], flattened[2][half_rows:])
    return jnp.concatenate([leading, trailing], axis=0).reshape(row_count, 1, heads_here, HEAD_DIM)


def head_product(attended, out_map, position, per_device):
    row_count = attended.shape[0]
    width_here = per_device * HEAD_DIM
    flattened = attended.reshape(row_count, width_here)
    map_rows = lax.dynamic_slice_in_dim(out_map, position * width_here, width_here, 0)
    return jnp.dot(flattened, map_rows, preferred_element_type=jnp.float32)


def local(query_rows, key_rows, value_rows, query_gain, key_gain, out_map, latents, step_index):
    query_normed = normalize(query_rows[0], query_gain)
    key_normed = normalize(key_rows[0], key_gain)
    value_local = value_rows[0]
    tok_rows = query_normed.shape[0]
    groups = lax.axis_size(("cfg", "seq"))
    per_device = HEADS // groups
    split_shape = (tok_rows, groups, per_device, HEAD_DIM)
    attended = attend_pair(
        (
            lax.all_to_all(
                query_normed.reshape(split_shape),
                ("cfg", "seq"),
                split_axis=1,
                concat_axis=0,
                tiled=True,
            ),
            lax.all_to_all(
                key_normed.reshape(split_shape),
                ("cfg", "seq"),
                split_axis=1,
                concat_axis=0,
                tiled=True,
            ),
            lax.all_to_all(
                value_local.reshape(split_shape),
                ("cfg", "seq"),
                split_axis=1,
                concat_axis=0,
                tiled=True,
            ),
        )
    )
    partial_value = head_product(attended, out_map, lax.axis_index(("cfg", "seq")), per_device)
    length = partial_value.shape[0] // 2
    weighted = GUIDANCE * partial_value[:length] + (1.0 - GUIDANCE) * partial_value[length:]
    summed = lax.psum_scatter(weighted, "seq", scatter_dimension=0, tiled=True)
    guided = lax.psum(summed, "cfg")
    progress = step_index[0].astype(jnp.float32)
    sigma_now = sigma_at(progress)
    sigma_next = sigma_at(progress + 1.0)
    return (latents + (sigma_next - sigma_now) * guided, latents - sigma_now * guided)


def solution(mesh):
    placed = (
        P("cfg", ("batch", "seq"), None),
        P("cfg", ("batch", "seq"), None),
        P("cfg", ("batch", "seq"), None),
        P(),
        P(),
        P(),
        P(("batch", "seq"), None),
        P(),
    )
    return jax.shard_map(
        local,
        mesh=mesh,
        in_specs=placed,
        out_specs=(P(("batch", "seq"), None), P(("batch", "seq"), None)),
        check_vma=False,
    )
```

profile of v0, /device:TPU:6, one launch (start us, length us, event | category | flops | bytes accessed | tf_op | source)
XLA Modules:
  0.0 259.3 jit_solution(9729841743482803806)
XLA Ops:
  7.2 3.6 %reshape.107 = f32[160,16,2,128]{3,2,1,0:T(2,128)S(1)} reshape(bf16[1,160,4096]{2,1,0:T(8,128)(2,1)} %param.12) | data formatting | bytes 3932160 | tf_op jit(solution)/shard_map/convert_element_type | solution.py:19
  10.8 1.7 multiply_reduce_fusion.3
  13.7 2.3 copy.34
  16.1 15.7 %all-to-all-start = ((bf16[160,16,2,128]{3,2,0,1:T(2,128)(2,1)}), bf16[160,16,2,128]{3,2,0,1:T(2,128)(2,1)}, u32[]{:S(2)}, u32[]{:S(2)}) async-start(bf16[160,16,2,128]{3,2,0,1:T(2,128)(2,1)} %copy.34), calls=%async_computation | async-start | bytes 2621440 | tf_op jit(solution)/shard_map/all_to_all | solution.py:86
  31.8 3.6 %reshape.108 = f32[160,16,2,128]{3,2,1,0:T(2,128)S(1)} reshape(bf16[1,160,4096]{2,1,0:T(8,128)(2,1)} %param.13) | data formatting | bytes 3932160 | tf_op jit(solution)/shard_map/convert_element_type | solution.py:19
  35.4 1.7 multiply_reduce_fusion.2
  39.9 29.2 %all-to-all-done = bf16[160,16,2,128]{3,2,0,1:T(2,128)(2,1)} async-done(((bf16[160,16,2,128]{3,2,0,1:T(2,128)(2,1)}), bf16[160,16,2,128]{3,2,0,1:T(2,128)(2,1)}, u32[]{:S(2)}, u32[]{:S(2)}) %all-to-all-start) | async-done | bytes 1310752 | tf_op jit(solution)/shard_map/all_to_all | solution.py:86
  69.1 11.4 %all-to-all-start.1 = ((bf16[160,16,2,128]{3,0,2,1:T(8,128)(2,1)}), bf16[160,16,2,128]{3,0,2,1:T(8,128)(2,1)S(1)}, u32[]{:S(2)}, u32[]{:S(2)}) async-start(bf16[160,16,2,128]{3,0,2,1:T(8,128)(2,1)} %copy.36), calls=%async_computation.1 | async-start | bytes 2621440 | tf_op jit(solution)/shard_map/all_to_all | solution.py:93
  80.5 3.6 %reshape_squeeze.3 = bf16[160,16,2,128]{3,2,1,0:T(2,128)(2,1)S(1)} reshape(bf16[1,160,4096]{2,1,0:T(8,128)(2,1)} %param.14) | data formatting | bytes 2621440 | tf_op jit(solution)/shard_map/reshape;squeeze | solution.py:101
  85.7 30.4 %all-to-all-done.1 = bf16[160,16,2,128]{3,0,2,1:T(8,128)(2,1)S(1)} async-done(((bf16[160,16,2,128]{3,0,2,1:T(8,128)(2,1)}), bf16[160,16,2,128]{3,0,2,1:T(8,128)(2,1)S(1)}, u32[]{:S(2)}, u32[]{:S(2)}) %all-to-all-start.1) | async-done | bytes 1310752 | tf_op jit(solution)/shard_map/all_to_all | solution.py:93
  116.1 10.6 %all-to-all-start.2 = ((bf16[160,16,2,128]{3,0,2,1:T(8,128)(2,1)}), bf16[160,16,2,128]{3,0,2,1:T(8,128)(2,1)S(1)}, u32[]{:S(2)}, u32[]{:S(2)}) async-start(bf16[160,16,2,128]{3,0,2,1:T(8,128)(2,1)} %copy.38), calls=%async_computation.2 | async-start | bytes 2621440 | tf_op jit(solution)/shard_map/all_to_all | solution.py:100
  130.2 32.7 %all-to-all-done.2 = bf16[160,16,2,128]{3,0,2,1:T(8,128)(2,1)S(1)} async-done(((bf16[160,16,2,128]{3,0,2,1:T(8,128)(2,1)}), bf16[160,16,2,128]{3,0,2,1:T(8,128)(2,1)S(1)}, u32[]{:S(2)}, u32[]{:S(2)}) %all-to-all-start.2) | async-done | bytes 1310752 | tf_op jit(solution)/shard_map/all_to_all | solution.py:100
  164.6 16.2 %while.20 = (s32[]{:T(128)}, bf16[2,640,2,128]{3,2,1,0:T(2,128)(2,1)S(1)}, bf16[2,640,2,128]{3,1,0,2:T(8,128)(2,1)S(1)}, bf16[1280,2,128]{2,0,1:T(8,128)(2,1)}, bf16[1280,2,128]{2,0,1:T(8,128)(2,1)}, /*index=5*/s32[]{:T(128)}) while((s32[]{:T(128)}, bf16[2,640,2,128]{3,2,1,0:T(2,128)(2,1)S(1)}, bf16[2,640,2,128]{3,1,0,2:T(8,128)(2,1)S(1)}, ...), condition=%wide.region_5.6_spmd, body=%wide.region_2.5_spmd.sunk | while | flops 1269927680 | bytes 3614801 | solution.py:54
  164.7 3.2 %fusion.115 = f32[2,640]{1,0:T(2,128)S(1)} fusion(bf16[1280,2,128]{2,0,1:T(8,128)(2,1)} %get-tuple-element.223, bf16[2,640,2,128]{3,1,0,2:T(8,128)(2,1)S(1)} %get-tuple-element.222, s32[]{:T(128)} %get-tuple-element.214), kind=kOutput, calls=%fused_computation.67.clone.1 | convolution fusion | flops 424346880 | bytes 988164 | tf_op jit(solution)/shard_map/while/body/eval_jaxpr/sub | solution.py:48
  168.0 4.4 %fusion.116 = bf16[1,640,2,128]{3,1,2,0:T(8,128)(2,1)S(1)} fusion(bf16[1280,2,128]{2,0,1:T(8,128)(2,1)} %get-tuple-element.224, f32[2,640]{1,0:T(2,128)S(1)} %fusion.115, bf16[1280,2,128]{2,0,1:T(8,128)(2,1)} %get-tuple-element.223, bf16[2,640,2,128]{3,1,0,2:T(8,128)(2,1)S(1)} %get-tuple-element.222, s32[]{:T(128)} %get-tuple-element.214), kind=kOutput, calls=%fused_computation.8.clone.1 | convolution fusion | flops 845580800 | bytes 1971204 | tf_op jit(solution)/shard_map/while/body/eval_jaxpr/hqk,khd->qhd/dot_general | solution.py:50
  172.8 3.2 %fusion.115 = f32[2,640]{1,0:T(2,128)S(1)} fusion(bf16[1280,2,128]{2,0,1:T(8,128)(2,1)} %get-tuple-element.223, bf16[2,640,2,128]{3,1,0,2:T(8,128)(2,1)S(1)} %get-tuple-element.222, s32[]{:T(128)} %get-tuple-element.214), kind=kOutput, calls=%fused_computation.67.clone.1 | convolution fusion | flops 424346880 | bytes 988164 | tf_op jit(solution)/shard_map/while/body/eval_jaxpr/sub | solution.py:48
  176.0 4.4 %fusion.116 = bf16[1,640,2,128]{3,1,2,0:T(8,128)(2,1)S(1)} fusion(bf16[1280,2,128]{2,0,1:T(8,128)(2,1)} %get-tuple-element.224, f32[2,640]{1,0:T(2,128)S(1)} %fusion.115, bf16[1280,2,128]{2,0,1:T(8,128)(2,1)} %get-tuple-element.223, bf16[2,640,2,128]{3,1,0,2:T(8,128)(2,1)S(1)} %get-tuple-element.222, s32[]{:T(128)} %get-tuple-element.214), kind=kOutput, calls=%fused_computation.8.clone.1 | convolution fusion | flops 845580800 | bytes 1971204 | tf_op jit(solution)/shard_map/while/body/eval_jaxpr/hqk,khd->qhd/dot_general | solution.py:50
  181.1 13.5 %while.21 = (s32[]{:T(128)}, bf16[2,640,2,128]{3,2,1,0:T(2,128)(2,1)S(1)}, bf16[2,640,2,128]{3,1,0,2:T(8,128)(2,1)S(1)}, bf16[1280,2,128]{2,0,1:T(8,128)(2,1)S(1)}, bf16[1280,2,128]{2,0,1:T(8,128)(2,1)}, /*index=5*/s32[]{:T(128)}) while((s32[]{:T(128)}, bf16[2,640,2,128]{3,2,1,0:T(2,128)(2,1)S(1)}, bf16[2,640,2,128]{3,1,0,2:T(8,128)(2,1)S(1)}, ...), condition=%wide.region_9.10_spmd, body=%wide.region_6.9_spmd.sunk | while | flops 1269927680 | bytes 3614801 | solution.py:54
  181.2 2.2 fusion.123
  183.3 4.2 %fusion.124 = bf16[1,640,2,128]{3,1,2,0:T(8,128)(2,1)S(1)} fusion(bf16[1280,2,128]{2,0,1:T(8,128)(2,1)} %get-tuple-element.206, f32[2,640]{1,0:T(2,128)S(1)} %fusion.123, bf16[1280,2,128]{2,0,1:T(8,128)(2,1)S(1)} %get-tuple-element.205, bf16[2,640,2,128]{3,1,0,2:T(8,128)(2,1)S(1)} %get-tuple-element.204, s32[]{:T(128)} %get-tuple-element.196), kind=kOutput, calls=%fused_computation.30.clone.1 | convolution fusion | flops 845580800 | bytes 1971204 | tf_op jit(solution)/shard_map/while/body/eval_jaxpr/hqk,khd->qhd/dot_general | solution.py:50
  187.9 2.2 fusion.123
  190.1 4.2 %fusion.124 = bf16[1,640,2,128]{3,1,2,0:T(8,128)(2,1)S(1)} fusion(bf16[1280,2,128]{2,0,1:T(8,128)(2,1)} %get-tuple-element.206, f32[2,640]{1,0:T(2,128)S(1)} %fusion.123, bf16[1280,2,128]{2,0,1:T(8,128)(2,1)S(1)} %get-tuple-element.205, bf16[2,640,2,128]{3,1,0,2:T(8,128)(2,1)S(1)} %get-tuple-element.204, s32[]{:T(128)} %get-tuple-element.196), kind=kOutput, calls=%fused_computation.30.clone.1 | convolution fusion | flops 845580800 | bytes 1971204 | tf_op jit(solution)/shard_map/while/body/eval_jaxpr/hqk,khd->qhd/dot_general | solution.py:50
  197.3 35.9 %reduce-scatter.4.cloned.1.call-done = f32[160,64]{1,0:T(8,128)} async-done(((f32[1280,64]{1,0:T(8,128)}), f32[160,64]{1,0:T(8,128)}) %reduce-scatter.4.cloned.1.call-update) | async-done | bytes 40976
  234.2 17.5 %psum.7 = f32[160,64]{0,1:T(8,128)S(1)} all-reduce(f32[160,64]{0,1:T(8,128)S(1)} %copy.45), channel_id=1, replica_groups=mesh['cfg'=2,'batch'=32,'seq'=8] {'cfg'}, use_global_device_ids=true, to_apply=%region_11.12 | all-reduce | flops 10240 | bytes 81920 | tf_op jit(solution)/shard_map/psum | solution.py:113
  (36 shorter events, 16.1 us)
Async XLA Ops:
  7.2 187.7 %copy-start = (bf16[4096,64]{0,1:T(8,128)(2,1)S(1)}, bf16[4096,64]{0,1:T(8,128)(2,1)}, u32[]{:S(2)}) copy-start(bf16[4096,64]{0,1:T(8,128)(2,1)} %param.17) | copy-start | bytes 1572868
  7.2 5.3 %copy-start.3 = (f32[4096]{0:T(1024)S(1)}, f32[4096]{0:T(1024)}, u32[]{:S(2)}) copy-start(f32[4096]{0:T(1024)} %param.15) | copy-start | bytes 49156
  16.1 53.0 %all-to-all-start = ((bf16[160,16,2,128]{3,2,0,1:T(2,128)(2,1)}), bf16[160,16,2,128]{3,2,0,1:T(2,128)(2,1)}, u32[]{:S(2)}, u32[]{:S(2)}) async-start(bf16[160,16,2,128]{3,2,0,1:T(2,128)(2,1)} %copy.34), calls=%async_computation | async-start | bytes 2621440 | tf_op jit(solution)/shard_map/all_to_all | solution.py:86
  31.8 5.3 %copy-start.4 = (f32[4096]{0:T(1024)S(1)}, f32[4096]{0:T(1024)}, u32[]{:S(2)}) copy-start(f32[4096]{0:T(1024)} %param.16) | copy-start | bytes 49156
  69.1 47.0 %all-to-all-start.1 = ((bf16[160,16,2,128]{3,0,2,1:T(8,128)(2,1)}), bf16[160,16,2,128]{3,0,2,1:T(8,128)(2,1)S(1)}, u32[]{:S(2)}, u32[]{:S(2)}) async-start(bf16[160,16,2,128]{3,0,2,1:T(8,128)(2,1)} %copy.36), calls=%async_computation.1 | async-start | bytes 2621440 | tf_op jit(solution)/shard_map/all_to_all | solution.py:93
  116.1 46.8 %all-to-all-start.2 = ((bf16[160,16,2,128]{3,0,2,1:T(8,128)(2,1)}), bf16[160,16,2,128]{3,0,2,1:T(8,128)(2,1)S(1)}, u32[]{:S(2)}, u32[]{:S(2)}) async-start(bf16[160,16,2,128]{3,0,2,1:T(8,128)(2,1)} %copy.38), calls=%async_computation.2 | async-start | bytes 2621440 | tf_op jit(solution)/shard_map/all_to_all | solution.py:100
  126.7 106.5 %reduce-scatter.4.cloned.1.call-start = ((), (), s32[]{:S(2)}) async-start(), calls=%async_computation.4 | async-start | bytes 737280
  163.0 1.5 copy-start.1
  194.9 56.9 %copy-start.2 = (f32[160,64]{0,1:T(8,128)S(1)}, f32[160,64]{0,1:T(8,128)}, u32[]{:S(2)}) copy-start(f32[160,64]{0,1:T(8,128)} %param.18) | copy-start | bytes 122884
Sparse Core Ops, SparseCore 0:
  196.7 36.5 reduce-scatter.3
where the time goes:
time: 260 us; the launch traced here: 259 us
  waiting for transfers between devices  128 us (49%)
  starting transfers between devices  37.8 us (15%)
  matrix products  28.5 us (11%)
  local copies, waits for them, and re-layouts  25.4 us (10%)
  blocking collectives  17.5 us (7%)
  between operations  15 us (6%)
  other arithmetic  6.55 us (3%)
    unnamed x2, waiting for transfers between devices  36 us
    all_to_all x1, waiting for transfers between devices, local(): lax.all_to_all(value_local.reshape(split_shape), ('cfg', 'seq'), split_ax...  32.7 us
    all_to_all x1, waiting for transfers between devices, local(): lax.all_to_all(key_normed.reshape(split_shape), ('cfg', 'seq'), split_axi...  30.4 us
    all_to_all x1, waiting for transfers between devices, local(): lax.all_to_all(query_normed.reshape(split_shape), ('cfg', 'seq'), split_a...  29.2 us
    psum x1, blocking collectives, local(): guided = lax.psum(summed, 'cfg')  17.5 us
    dot_general x4, matrix products, one_block(): jnp.einsum('hqk,khd->qhd', weights_bf, value_part, preferred_element_type...  17.2 us
    all_to_all x1, starting transfers between devices, local(): lax.all_to_all(query_normed.reshape(split_shape), ('cfg', 'seq'), split_a...  15.7 us
    all_to_all x1, starting transfers between devices, local(): lax.all_to_all(key_normed.reshape(split_shape), ('cfg', 'seq'), split_axi...  11.4 us
  transfers between devices with their start and end apart: 4, of which 4 were waited for; matrix products, arithmetic and copies ran while one was open for 6% of the time, Pallas kernels for 0%

commit v1 on v0

v1 whole, which is shorter than its diff:
```python
import functools
import math

import jax
import jax.numpy as jnp
from jax import lax
from jax.experimental import pallas as pl
from jax.experimental.pallas import tpu as pltpu
from jax.sharding import PartitionSpec as P

HEADS = 32
HEAD_DIM = 128
CHANNELS = 64
STEPS = 50
GUIDANCE = 5.0
FLOW_SHIFT = 5.0
EPSILON = 1e-06
VMEM_LIMIT = 48 * 1024 * 1024


def sigma_at(progress):
    remain = 1.0 - progress / STEPS
    return FLOW_SHIFT * remain / (1.0 + (FLOW_SHIFT - 1.0) * remain)


def params():
    return pltpu.CompilerParams(vmem_limit_bytes=VMEM_LIMIT)


def normed(rows_ref, gain_ref):
    values = rows_ref[...].astype(jnp.float32)
    mean_square = jnp.mean(values * values, axis=-1, keepdims=True)
    return (values * lax.rsqrt(mean_square + EPSILON) * gain_ref[...]).astype(jnp.bfloat16)


def pack_kv_kernel(groups, key_ref, value_ref, gain_ref, map_ref, out_ref):
    width = key_ref.shape[1] // groups
    key_normed = normed(key_ref, gain_ref)
    pair = 2 * HEAD_DIM
    row = lax.broadcasted_iota(jnp.int32, (pair, 2 * CHANNELS), 0)
    lane = lax.broadcasted_iota(jnp.int32, (pair, 2 * CHANNELS), 1)
    same_head = (row < HEAD_DIM) == (lane < CHANNELS)
    for group in range(groups):
        out_ref[group, :, :width] = key_normed[:, group * width : (group + 1) * width]
        for step in range(width // pair):
            first = group * width + step * pair
            columns = map_ref[first : first + pair, :]
            both = jnp.concatenate([columns, columns], axis=1)
            both = jnp.where(same_head, both, jnp.zeros_like(both))
            mapped = jnp.dot(
                value_ref[:, first : first + pair], both, preferred_element_type=jnp.float32
            )
            left = width + step * 2 * CHANNELS
            out_ref[group, :, left : left + 2 * CHANNELS] = mapped.astype(jnp.bfloat16)


def pack_kv(key_rows, value_rows, gain, out_map, groups, blocks=2):
    rows, features = key_rows.shape
    width = features // groups
    packed = width + width // HEAD_DIM * CHANNELS
    step = rows // blocks
    return pl.pallas_call(
        functools.partial(pack_kv_kernel, groups),
        out_shape=jax.ShapeDtypeStruct((groups, rows, packed), jnp.bfloat16),
        grid=(blocks,),
        in_specs=[
            pl.BlockSpec((step, features), lambda i: (i, 0)),
            pl.BlockSpec((step, features), lambda i: (i, 0)),
            pl.BlockSpec((1, features), lambda i: (0, 0)),
            pl.BlockSpec((features, CHANNELS), lambda i: (0, 0)),
        ],
        out_specs=pl.BlockSpec((groups, step, packed), lambda i: (0, i, 0)),
        compiler_params=params(),
        cost_estimate=pl.CostEstimate(flops=2**28, bytes_accessed=5 * 2**20, transcendentals=0),
        name="pack_kv",
    )(key_rows, value_rows, gain, out_map)


def pack_q_kernel(groups, place_ref, query_ref, gain_ref, *refs):
    out_refs, scratch = refs[:groups], refs[groups]
    width = query_ref.shape[1] // groups
    scratch[...] = normed(query_ref, gain_ref)
    place = place_ref[0]
    for e in range(groups):
        first = pl.multiple_of(jnp.bitwise_xor(place, e) * width, width)
        out_refs[e][...] = scratch[:, pl.ds(first, width)]


def pack_q(place, query_rows, gain, groups, blocks=2):
    rows, features = query_rows.shape
    width = features // groups
    step = rows // blocks
    return pl.pallas_call(
        functools.partial(pack_q_kernel, groups),
        out_shape=[jax.ShapeDtypeStruct((rows, width), jnp.bfloat16)] * groups,
        grid=(blocks,),
        in_specs=[
            pl.BlockSpec(memory_space=pltpu.SMEM),
            pl.BlockSpec((step, features), lambda i: (i, 0)),
            pl.BlockSpec((1, features), lambda i: (0, 0)),
        ],
        out_specs=[pl.BlockSpec((step, width), lambda i: (i, 0))] * groups,
        scratch_shapes=[pltpu.VMEM((step, features), jnp.bfloat16)],
        compiler_params=params(),
        cost_estimate=pl.CostEstimate(flops=2**24, bytes_accessed=5 * 2**19, transcendentals=0),
        name="pack_q",
    )(place, query_rows, gain)


def attend_kernel(count, *refs):
    query_refs, kv_ref, out_ref = refs[:count], refs[count], refs[count + 1]
    width = query_refs[0].shape[1]
    rows = query_refs[0].shape[0]
    factor = math.log2(math.e) / math.sqrt(HEAD_DIM)
    left_half = lax.broadcasted_iota(jnp.int32, (1, 2 * CHANNELS), 1) < CHANNELS
    for block in range(count):
        total = None
        for pair in range(width // (2 * HEAD_DIM)):
            terms = []
            for head in (2 * pair, 2 * pair + 1):
                lanes = slice(head * HEAD_DIM, (head + 1) * HEAD_DIM)
                scores = lax.dot_general(
                    query_refs[block][:, lanes],
                    kv_ref[:, lanes],
                    (((1,), (1,)), ((), ())),
                    preferred_element_type=jnp.float32,
                )
                top = jnp.max(scores, axis=-1, keepdims=True)
                weights = jnp.exp2((scores - top) * factor)
                inverse = 1.0 / jnp.sum(weights, axis=-1, keepdims=True)
                left = width + pair * 2 * CHANNELS
                terms.append(
                    jnp.dot(
                        (weights * inverse).astype(jnp.bfloat16),
                        kv_ref[:, left : left + 2 * CHANNELS],
                        preferred_element_type=jnp.float32,
                    )
                )
            term = jnp.where(left_half, terms[0], terms[1])
            total = term if total is None else total + term
        total = total + pltpu.roll(total, CHANNELS, 1)
        half = rows // 2
        out_ref[block] = jnp.where(left_half, total[:half], total[half:])


def attend(queries, kv):
    count = len(queries)
    rows, width = queries[0].shape
    keys = kv.shape[0]
    work = count * rows * keys * (width // HEAD_DIM)
    return pl.pallas_call(
        functools.partial(attend_kernel, count),
        out_shape=jax.ShapeDtypeStruct((count, rows // 2, 2 * CHANNELS), jnp.float32),
        in_specs=[pl.BlockSpec(memory_space=pltpu.VMEM)] * (count + 1),
        out_specs=pl.BlockSpec(memory_space=pltpu.VMEM),
        compiler_params=params(),
        cost_estimate=pl.CostEstimate(
            flops=work * 4 * HEAD_DIM, bytes_accessed=2 * kv.size, transcendentals=work
        ),
        name="attend",
    )(*queries, kv)


def local(query_rows, key_rows, value_rows, query_gain, key_gain, out_map, latents, step_index):
    groups = lax.axis_size("seq")
    place = lax.axis_index("seq").astype(jnp.int32).reshape(1)
    rows = query_rows.shape[1]

    def exchange(array, e):
        return lax.ppermute(array, "seq", [(i, i ^ e) for i in range(groups)])

    kv_mine = pack_kv(key_rows[0], value_rows[0], key_gain.reshape(1, -1), out_map, groups)
    kv = lax.all_to_all(kv_mine, "seq", split_axis=0, concat_axis=0, tiled=True)
    kv = kv.reshape(groups * rows, kv.shape[2])
    query_parts = pack_q(place, query_rows[0], query_gain.reshape(1, -1), groups)
    held = {0: query_parts[0]}
    for e in (4, 5, 6, 7, 3, 2, 1):
        held[e] = exchange(query_parts[e], e)

    own = attend([held[0]], kv)[0]
    far = [attend([held[e]], kv) for e in (4, 5, 6, 7)]
    from_far = exchange(jnp.concatenate(far, axis=0), 4)
    second = [attend([held[e]], kv)[0] for e in (2, 3)]
    from_second = exchange(
        jnp.stack([second[0] + from_far[2], second[1] + from_far[3]]), 2
    )
    last = attend([held[1]], kv)[0]
    from_last = exchange(last + from_far[1] + from_second[1], 1)
    total = own + from_far[0] + from_second[0] + from_last

    share = jnp.where(lax.axis_index("cfg") == 0, GUIDANCE, 1.0 - GUIDANCE)
    total = total * share
    total = total + lax.ppermute(total, "cfg", [(0, 1), (1, 0)])
    guided = jnp.concatenate([total[:, :CHANNELS], total[:, CHANNELS:]], axis=0)

    progress = step_index[0].astype(jnp.float32)
    sigma_now = sigma_at(progress)
    sigma_next = sigma_at(progress + 1.0)
    return (latents + (sigma_next - sigma_now) * guided, latents - sigma_now * guided)


def solution(mesh):
    placed = (
        P("cfg", ("batch", "seq"), None),
        P("cfg", ("batch", "seq"), None),
        P("cfg", ("batch", "seq"), None),
        P(),
        P(),
        P(),
        P(("batch", "seq"), None),
        P(),
    )
    return jax.shard_map(
        local,
        mesh=mesh,
        in_specs=placed,
        out_specs=(P(("batch", "seq"), None), P(("batch", "seq"), None)),
        check_vma=False,
    )
```

time: 260 us -> 135 us (0.52)
  waiting for transfers between devices: 128 us -> 38.6 us
  matrix products: 28.5 us -> 0 us
  starting transfers between devices: 37.8 us -> 63.6 us
  Pallas kernels: 0 us -> 22.9 us
  local copies, waits for them, and re-layouts: 25.4 us -> 6.51 us
  blocking collectives: 17.5 us -> 0 us
  between operations: 15 us -> 1.76 us
  other arithmetic: 6.55 us -> 0.1 us
    all_to_all x3 -> x1, waiting for transfers between devices: 92.3 us -> 0.63 us  [local(): kv = lax.all_to_all(kv_mine, 'seq', split_axis=0, concat_axis=0, tiled=True)]
    ppermute x0 -> x11, starting transfers between devices: none -> 56.4 us  [the longest x10 45.5 us: exchange(): return lax.ppermute(array, 'seq', [(i, i ^ e) for i in range(groups)])]
    ppermute x0 -> x11, waiting for transfers between devices: none -> 37.9 us  [the longest x10 36.8 us: exchange(): return lax.ppermute(array, 'seq', [(i, i ^ e) for i in range(groups)])]
    unnamed x2 -> x0, waiting for transfers between devices: 36 us -> none
    all_to_all x3 -> x1, starting transfers between devices: 37.8 us -> 7.23 us  [local(): kv = lax.all_to_all(kv_mine, 'seq', split_axis=0, concat_axis=0, tiled=True)]
    pallas_call x0 -> x10, Pallas kernels: none -> 22.9 us  [the longest x8 19.7 us: attend(): pl.pallas_call(functools.partial(attend_kernel, count), out_shape=jax.Sha...]
    dot_general x5 -> x0, matrix products: 17.7 us -> none  [the longest x4 17.2 us: one_block(): jnp.einsum('hqk,khd->qhd', weights_bf, value_part, preferred_element_type...]
    psum x1 -> x0, blocking collectives: 17.5 us -> none  [local(): guided = lax.psum(summed, 'cfg')]
  transfers between devices with their start and end apart: 4 -> 12, of which waited for: 4 -> 5; matrix products, arithmetic and copies ran while one was open for 6% -> 0% of each run, Pallas kernels for 0% -> 16%
where the time goes in v1:
time: 135 us; the launch traced here: 133 us
  starting transfers between devices  63.6 us (47%)
  waiting for transfers between devices  38.6 us (29%)
  Pallas kernels  22.9 us (17%)
  local copies, waits for them, and re-layouts  6.51 us (5%)
  between operations  1.76 us (1%)
    ppermute x10, starting transfers between devices, exchange(): return lax.ppermute(array, 'seq', [(i, i ^ e) for i in range(groups)])  45.5 us
    ppermute x10, waiting for transfers between devices, exchange(): return lax.ppermute(array, 'seq', [(i, i ^ e) for i in range(groups)])  36.8 us
    pallas_call x8, Pallas kernels, attend(): pl.pallas_call(functools.partial(attend_kernel, count), out_shape=jax.Sha...  19.7 us
    ppermute x1, starting transfers between devices, local(): total = total + lax.ppermute(total, 'cfg', [(0, 1), (1, 0)])  10.9 us
    all_to_all x1, starting transfers between devices, local(): kv = lax.all_to_all(kv_mine, 'seq', split_axis=0, concat_axis=0, tiled=True)  7.23 us
    unnamed x22, local copies, waits for them, and re-layouts  6.43 us
  transfers between devices with their start and end apart: 12, of which 5 were waited for; matrix products, arithmetic and copies ran while one was open for 0% of the time, Pallas kernels for 16%

profile of v1, /device:TPU:6, one launch (start us, length us, event | category | flops | bytes accessed | tf_op | source)
XLA Modules:
  0.0 133.4 jit_solution(9283955763744998560)
XLA Ops:
  0.7 1.6 %copy.10.map_ref = bf16[4096,64]{1,0:T(8,128)(2,1)S(1)} copy(bf16[4096,64]{0,1:T(8,128)(2,1)} %param.13) | data formatting | bytes 1048576 | tf_op args[5]
  6.5 7.2 %all-to-all-start = ((bf16[8,160,768]{2,1,0:T(8,128)(2,1)}), bf16[8,160,768]{2,1,0:T(8,128)(2,1)S(1)}, u32[]{:S(2)}, u32[]{:S(2)}) async-start(bf16[8,160,768]{2,1,0:T(8,128)(2,1)} %copy-done), calls=%async_computation | async-start | bytes 3932160 | tf_op jit(solution)/shard_map/all_to_all | solution.py:173
  13.7 1.6 %pack_q.1 = (bf16[160,512]{1,0:T(8,128)(2,1)S(1)}, bf16[160,512]{1,0:T(8,128)(2,1)S(1)}, bf16[160,512]{1,0:T(8,128)(2,1)}, bf16[160,512]{1,0:T(8,128)(2,1)}, bf1...) custom-call(s32[1]{0:T(128)} %bitcast.2.place_ref, ...), custom_call_target="tpu_custom_call" | custom-call | flops 16777216 | bytes 2621440 | tf_op jit(solution)/shard_map/pack_q/pallas_call | solution.py:93
  16.0 7.8 %collective-permute-start = (bf16[160,512]{1,0:T(8,128)(2,1)S(1)}, bf16[160,512]{1,0:T(8,128)(2,1)S(1)}, u32[]{:S(2)}, u32[]{:S(2)}) collective-permute-start(bf16[160,512]{1,0:T(8,128)(2,1)S(1)} %get-tuple-element.11), channel_id=1, source_target_pairs={{0,4},{1,5},{2,6},{3,7},{4,0},{5,1},{6,2},{7,3},{8,12},{9,13},{10,... | collective-permute-start | bytes 491528 | tf_op jit(solution)/shard_map/ppermute | solution.py:170
  23.8 2.5 %collective-permute-start.1 = (bf16[160,512]{1,0:T(8,128)(2,1)}, bf16[160,512]{1,0:T(8,128)(2,1)S(1)}, u32[]{:S(2)}, u32[]{:S(2)}) collective-permute-start(bf16[160,512]{1,0:T(8,128)(2,1)} %get-tuple-element.12), channel_id=1, source_target_pairs={{0,5},{1,4},{2,7},{3,6},{4,1},{5,0},{6,3},{7,2},{8,13},{9,12},{10,... | collective-permute-start | bytes 491528 | tf_op jit(solution)/shard_map/ppermute | solution.py:170
  26.3 4.6 %collective-permute-start.2 = (bf16[160,512]{1,0:T(8,128)(2,1)}, bf16[160,512]{1,0:T(8,128)(2,1)S(1)}, u32[]{:S(2)}, u32[]{:S(2)}) collective-permute-start(bf16[160,512]{1,0:T(8,128)(2,1)} %get-tuple-element.13), channel_id=1, source_target_pairs={{0,6},{1,7},{2,4},{3,5},{4,2},{5,3},{6,0},{7,1},{8,14},{9,15},{10,... | collective-permute-start | bytes 491528 | tf_op jit(solution)/shard_map/ppermute | solution.py:170
  30.9 1.9 %collective-permute-start.3 = (bf16[160,512]{1,0:T(8,128)(2,1)}, bf16[160,512]{1,0:T(8,128)(2,1)S(1)}, u32[]{:S(2)}, u32[]{:S(2)}) collective-permute-start(bf16[160,512]{1,0:T(8,128)(2,1)} %get-tuple-element.14), channel_id=1, source_target_pairs={{0,7},{1,6},{2,5},{3,4},{4,3},{5,2},{6,1},{7,0},{8,15},{9,14},{10,... | collective-permute-start | bytes 491528 | tf_op jit(solution)/shard_map/ppermute | solution.py:170
  32.8 5.7 %collective-permute-start.5 = (bf16[160,512]{1,0:T(8,128)(2,1)}, bf16[160,512]{1,0:T(8,128)(2,1)S(1)}, u32[]{:S(2)}, u32[]{:S(2)}) collective-permute-start(bf16[160,512]{1,0:T(8,128)(2,1)} %get-tuple-element.15), channel_id=1, source_target_pairs={{0,2},{1,3},{2,0},{3,1},{4,6},{5,7},{6,4},{7,5},{8,10},{9,11},{10,... | collective-permute-start | bytes 491528 | tf_op jit(solution)/shard_map/ppermute | solution.py:170
  38.6 31.2 %collective-permute-done.refs_0_ = bf16[160,512]{1,0:T(8,128)(2,1)S(1)} collective-permute-done((bf16[160,512]{1,0:T(8,128)(2,1)S(1)}, bf16[160,512]{1,0:T(8,128)(2,1)S(1)}, u32[]{:S(2)}, u32[]{:S(2)}) %collective-permute-start) | collective-permute-done | bytes 163872 | tf_op jit(solution)/shard_map/ppermute | solution.py:170
  69.8 4.1 %collective-permute-start.6 = (bf16[160,512]{1,0:T(8,128)(2,1)}, bf16[160,512]{1,0:T(8,128)(2,1)S(1)}, u32[]{:S(2)}, u32[]{:S(2)}) collective-permute-start(bf16[160,512]{1,0:T(8,128)(2,1)} %get-tuple-element.16), channel_id=1, source_target_pairs={{0,3},{1,2},{2,1},{3,0},{4,7},{5,6},{6,5},{7,4},{8,11},{9,10},{10,... | collective-permute-start | bytes 491528 | tf_op jit(solution)/shard_map/ppermute | solution.py:170
  74.5 2.5 %attend.9 = f32[1,80,128]{2,1,0:T(8,128)S(1)} custom-call(bf16[160,512]{1,0:T(8,128)(2,1)S(1)} %collective-permute-done.refs_0_, bf16[1280,768]{1,0:T(8,128)(2,1)S(1)} %bitcast.17), custom_call_target="tpu_custom_call" | custom-call | flops 419430400 | bytes 1966080 | tf_op jit(solution)/shard_map/attend/pallas_call | solution.py:151
  77.0 4.7 %collective-permute-done.1.refs_0_ = bf16[160,512]{1,0:T(8,128)(2,1)S(1)} collective-permute-done((bf16[160,512]{1,0:T(8,128)(2,1)}, bf16[160,512]{1,0:T(8,128)(2,1)S(1)}, u32[]{:S(2)}, u32[]{:S(2)}) %collective-permute-start.1) | collective-permute-done | bytes 163872 | tf_op jit(solution)/shard_map/ppermute | solution.py:170
  81.7 2.5 %attend.10 = f32[1,80,128]{2,1,0:T(8,128)S(1)} custom-call(bf16[160,512]{1,0:T(8,128)(2,1)S(1)} %collective-permute-done.1.refs_0_, bf16[1280,768]{1,0:T(8,128)(2,1)S(1)} %bitcast.18), custom_call_target="tpu_custom_call" | custom-call | flops 419430400 | bytes 1966080 | tf_op jit(solution)/shard_map/attend/pallas_call | solution.py:151
  84.1 2.5 %attend.11 = f32[1,80,128]{2,1,0:T(8,128)S(1)} custom-call(bf16[160,512]{1,0:T(8,128)(2,1)S(1)} %collective-permute-done.2.refs_0_, bf16[1280,768]{1,0:T(8,128)(2,1)S(1)} %bitcast.19), custom_call_target="tpu_custom_call" | custom-call | flops 419430400 | bytes 1966080 | tf_op jit(solution)/shard_map/attend/pallas_call | solution.py:151
  87.5 2.5 %attend.12 = f32[1,80,128]{2,1,0:T(8,128)S(1)} custom-call(bf16[160,512]{1,0:T(8,128)(2,1)S(1)} %collective-permute-done.3.refs_0_, bf16[1280,768]{1,0:T(8,128)(2,1)S(1)} %bitcast.20), custom_call_target="tpu_custom_call" | custom-call | flops 419430400 | bytes 1966080 | tf_op jit(solution)/shard_map/attend/pallas_call | solution.py:151
  90.0 5.2 %collective-permute-start.4 = (f32[4,80,128]{2,1,0:T(8,128)S(1)}, f32[4,80,128]{2,1,0:T(8,128)S(1)}, u32[]{:S(2)}, u32[]{:S(2)}) collective-permute-start(f32[4,80,128]{2,1,0:T(8,128)S(1)} %pad_maximum_fusion), channel_id=1, source_target_pairs={{0,4},{1,5},{2,6},{3,7},{4,0},{5,1},{6,2},{7,3},{8,12},{9,13},{10,... | collective-permute-start | bytes 491528 | tf_op jit(solution)/shard_map/ppermute | solution.py:170
  95.2 3.8 %collective-permute-start.8 = (bf16[160,512]{1,0:T(8,128)(2,1)S(1)}, bf16[160,512]{1,0:T(8,128)(2,1)S(1)}, u32[]{:S(2)}, u32[]{:S(2)}) collective-permute-start(bf16[160,512]{1,0:T(8,128)(2,1)S(1)} %copy-done.7), channel_id=1, source_target_pairs={{0,1},{1,0},{2,3},{3,2},{4,5},{5,4},{6,7},{7,6},{8,9},{9,8},{10,11... | collective-permute-start | bytes 491528 | tf_op jit(solution)/shard_map/ppermute | solution.py:170
  99.0 2.5 %attend.13 = f32[1,80,128]{2,1,0:T(8,128)S(1)} custom-call(bf16[160,512]{1,0:T(8,128)(2,1)S(1)} %collective-permute-done.5.refs_0_, bf16[1280,768]{1,0:T(8,128)(2,1)S(1)} %bitcast.21), custom_call_target="tpu_custom_call" | custom-call | flops 419430400 | bytes 1966080 | tf_op jit(solution)/shard_map/attend/pallas_call | solution.py:151
  101.5 2.5 %attend.14 = f32[1,80,128]{2,1,0:T(8,128)S(1)} custom-call(bf16[160,512]{1,0:T(8,128)(2,1)S(1)} %collective-permute-done.6.refs_0_, bf16[1280,768]{1,0:T(8,128)(2,1)S(1)} %bitcast.22), custom_call_target="tpu_custom_call" | custom-call | flops 419430400 | bytes 1966080 | tf_op jit(solution)/shard_map/attend/pallas_call | solution.py:151
  104.0 6.2 %collective-permute-start.7 = (f32[2,80,128]{2,1,0:T(8,128)S(1)}, f32[2,80,128]{2,1,0:T(8,128)S(1)}, u32[]{:S(2)}, u32[]{:S(2)}) collective-permute-start(f32[2,80,128]{2,1,0:T(8,128)S(1)} %pad_maximum_fusion.1), channel_id=1, source_target_pairs={{0,2},{1,3},{2,0},{3,1},{4,6},{5,7},{6,4},{7,5},{8,10},{9,11},{10,... | collective-permute-start | bytes 245768 | tf_op jit(solution)/shard_map/ppermute | solution.py:170
  110.2 2.5 %attend.15 = f32[1,80,128]{2,1,0:T(8,128)S(1)} custom-call(bf16[160,512]{1,0:T(8,128)(2,1)S(1)} %collective-permute-done.8.refs_0_, bf16[1280,768]{1,0:T(8,128)(2,1)S(1)} %bitcast.23), custom_call_target="tpu_custom_call" | custom-call | flops 419430400 | bytes 1966080 | tf_op jit(solution)/shard_map/attend/pallas_call | solution.py:151
  112.7 3.7 %collective-permute-start.9 = (f32[80,128]{1,0:T(8,128)S(1)}, f32[80,128]{1,0:T(8,128)S(1)}, u32[]{:S(2)}, u32[]{:S(2)}) collective-permute-start(f32[80,128]{1,0:T(8,128)S(1)} %fusion), channel_id=1, source_target_pairs={{0,1},{1,0},{2,3},{3,2},{4,5},{5,4},{6,7},{7,6},{8,9},{9,8},{10,11... | collective-permute-start | bytes 122888 | tf_op jit(solution)/shard_map/ppermute | solution.py:170
  116.4 2.5 %attend.8 = f32[1,80,128]{2,1,0:T(8,128)S(1)} custom-call(bf16[160,512]{1,0:T(8,128)(2,1)S(1)} %get-tuple-element.10.refs_0_, bf16[1280,768]{1,0:T(8,128)(2,1)S(1)} %bitcast.24), custom_call_target="tpu_custom_call" | custom-call | flops 419430400 | bytes 1966080 | tf_op jit(solution)/shard_map/attend/pallas_call | solution.py:151
  118.9 10.9 %collective-permute-start.10 = (f32[80,128]{1,0:T(8,128)S(1)}, f32[80,128]{1,0:T(8,128)S(1)}, u32[]{:S(2)}, u32[]{:S(2)}) collective-permute-start(f32[80,128]{1,0:T(8,128)S(1)} %fusion.3), channel_id=1, source_target_pairs={{0,256},{256,0},{1,257},{257,1},{2,258},{258,2},{3,259},{259,3},{4... | collective-permute-start | bytes 122888 | tf_op jit(solution)/shard_map/ppermute | solution.py:193
  (40 shorter events, 9.2 us)
Async XLA Ops:
  0.6 1.6 %copy-start.4 = (f32[4096]{0:T(1024)S(1)}, f32[4096]{0:T(1024)}, u32[]{:S(2)}) copy-start(f32[4096]{0:T(1024)} %param.12) | copy-start | bytes 49156
  0.6 1.6 %copy-start.2 = (bf16[1,160,4096]{2,1,0:T(8,128)(2,1)S(1)}, bf16[1,160,4096]{2,1,0:T(8,128)(2,1)}, u32[]{:S(2)}) copy-start(bf16[1,160,4096]{2,1,0:T(8,128)(2,1)} %param.9) | copy-start | bytes 3932164
  2.3 1.3 copy-start.3
  5.2 1.3 copy-start
  6.5 7.2 %copy-start.1 = (bf16[1,160,4096]{2,1,0:T(8,128)(2,1)S(1)}, bf16[1,160,4096]{2,1,0:T(8,128)(2,1)}, u32[]{:S(2)}) copy-start(bf16[1,160,4096]{2,1,0:T(8,128)(2,1)} %param.8) | copy-start | bytes 3932164
  6.5 7.2 %copy-start.5 = (f32[4096]{0:T(1024)S(1)}, f32[4096]{0:T(1024)}, u32[]{:S(2)}) copy-start(f32[4096]{0:T(1024)} %param.11) | copy-start | bytes 49156
  6.5 68.0 %all-to-all-start = ((bf16[8,160,768]{2,1,0:T(8,128)(2,1)}), bf16[8,160,768]{2,1,0:T(8,128)(2,1)S(1)}, u32[]{:S(2)}, u32[]{:S(2)}) async-start(bf16[8,160,768]{2,1,0:T(8,128)(2,1)} %copy-done), calls=%async_computation | async-start | bytes 3932160 | tf_op jit(solution)/shard_map/all_to_all | solution.py:173
  15.4 0.7 copy-start.6
  16.0 53.8 %collective-permute-start = (bf16[160,512]{1,0:T(8,128)(2,1)S(1)}, bf16[160,512]{1,0:T(8,128)(2,1)S(1)}, u32[]{:S(2)}, u32[]{:S(2)}) collective-permute-start(bf16[160,512]{1,0:T(8,128)(2,1)S(1)} %get-tuple-element.11), channel_id=1, source_target_pairs={{0,4},{1,5},{2,6},{3,7},{4,0},{5,1},{6,2},{7,3},{8,12},{9,13},{10,... | collective-permute-start | bytes 491528 | tf_op jit(solution)/shard_map/ppermute | solution.py:170
  23.8 57.8 %collective-permute-start.1 = (bf16[160,512]{1,0:T(8,128)(2,1)}, bf16[160,512]{1,0:T(8,128)(2,1)S(1)}, u32[]{:S(2)}, u32[]{:S(2)}) collective-permute-start(bf16[160,512]{1,0:T(8,128)(2,1)} %get-tuple-element.12), channel_id=1, source_target_pairs={{0,5},{1,4},{2,7},{3,6},{4,1},{5,0},{6,3},{7,2},{8,13},{9,12},{10,... | collective-permute-start | bytes 491528 | tf_op jit(solution)/shard_map/ppermute | solution.py:170
  26.3 57.8 %collective-permute-start.2 = (bf16[160,512]{1,0:T(8,128)(2,1)}, bf16[160,512]{1,0:T(8,128)(2,1)S(1)}, u32[]{:S(2)}, u32[]{:S(2)}) collective-permute-start(bf16[160,512]{1,0:T(8,128)(2,1)} %get-tuple-element.13), channel_id=1, source_target_pairs={{0,6},{1,7},{2,4},{3,5},{4,2},{5,3},{6,0},{7,1},{8,14},{9,15},{10,... | collective-permute-start | bytes 491528 | tf_op jit(solution)/shard_map/ppermute | solution.py:170
  30.9 56.6 %collective-permute-start.3 = (bf16[160,512]{1,0:T(8,128)(2,1)}, bf16[160,512]{1,0:T(8,128)(2,1)S(1)}, u32[]{:S(2)}, u32[]{:S(2)}) collective-permute-start(bf16[160,512]{1,0:T(8,128)(2,1)} %get-tuple-element.14), channel_id=1, source_target_pairs={{0,7},{1,6},{2,5},{3,4},{4,3},{5,2},{6,1},{7,0},{8,15},{9,14},{10,... | collective-permute-start | bytes 491528 | tf_op jit(solution)/shard_map/ppermute | solution.py:170
  32.8 66.2 %collective-permute-start.5 = (bf16[160,512]{1,0:T(8,128)(2,1)}, bf16[160,512]{1,0:T(8,128)(2,1)S(1)}, u32[]{:S(2)}, u32[]{:S(2)}) collective-permute-start(bf16[160,512]{1,0:T(8,128)(2,1)} %get-tuple-element.15), channel_id=1, source_target_pairs={{0,2},{1,3},{2,0},{3,1},{4,6},{5,7},{6,4},{7,5},{8,10},{9,11},{10,... | collective-permute-start | bytes 491528 | tf_op jit(solution)/shard_map/ppermute | solution.py:170
  69.8 31.7 %collective-permute-start.6 = (bf16[160,512]{1,0:T(8,128)(2,1)}, bf16[160,512]{1,0:T(8,128)(2,1)S(1)}, u32[]{:S(2)}, u32[]{:S(2)}) collective-permute-start(bf16[160,512]{1,0:T(8,128)(2,1)} %get-tuple-element.16), channel_id=1, source_target_pairs={{0,3},{1,2},{2,1},{3,0},{4,7},{5,6},{6,5},{7,4},{8,11},{9,10},{10,... | collective-permute-start | bytes 491528 | tf_op jit(solution)/shard_map/ppermute | solution.py:170
  86.6 8.6 %copy-start.7 = (bf16[160,512]{1,0:T(8,128)(2,1)S(1)}, bf16[160,512]{1,0:T(8,128)(2,1)}, u32[]{:S(2)}) copy-start(bf16[160,512]{1,0:T(8,128)(2,1)} %copy-done.6) | copy-start | bytes 491524
  90.0 14.0 %collective-permute-start.4 = (f32[4,80,128]{2,1,0:T(8,128)S(1)}, f32[4,80,128]{2,1,0:T(8,128)S(1)}, u32[]{:S(2)}, u32[]{:S(2)}) collective-permute-start(f32[4,80,128]{2,1,0:T(8,128)S(1)} %pad_maximum_fusion), channel_id=1, source_target_pairs={{0,4},{1,5},{2,6},{3,7},{4,0},{5,1},{6,2},{7,3},{8,12},{9,13},{10,... | collective-permute-start | bytes 491528 | tf_op jit(solution)/shard_map/ppermute | solution.py:170
  95.2 15.0 %collective-permute-start.8 = (bf16[160,512]{1,0:T(8,128)(2,1)S(1)}, bf16[160,512]{1,0:T(8,128)(2,1)S(1)}, u32[]{:S(2)}, u32[]{:S(2)}) collective-permute-start(bf16[160,512]{1,0:T(8,128)(2,1)S(1)} %copy-done.7), channel_id=1, source_target_pairs={{0,1},{1,0},{2,3},{3,2},{4,5},{5,4},{6,7},{7,6},{8,9},{9,8},{10,11... | collective-permute-start | bytes 491528 | tf_op jit(solution)/shard_map/ppermute | solution.py:170
  104.0 8.7 %collective-permute-start.7 = (f32[2,80,128]{2,1,0:T(8,128)S(1)}, f32[2,80,128]{2,1,0:T(8,128)S(1)}, u32[]{:S(2)}, u32[]{:S(2)}) collective-permute-start(f32[2,80,128]{2,1,0:T(8,128)S(1)} %pad_maximum_fusion.1), channel_id=1, source_target_pairs={{0,2},{1,3},{2,0},{3,1},{4,6},{5,7},{6,4},{7,5},{8,10},{9,11},{10,... | collective-permute-start | bytes 245768 | tf_op jit(solution)/shard_map/ppermute | solution.py:170
  112.7 17.9 %copy-start.8 = (f32[160,64]{0,1:T(8,128)S(1)}, f32[160,64]{0,1:T(8,128)}, u32[]{:S(2)}) copy-start(f32[160,64]{0,1:T(8,128)} %param.14) | copy-start | bytes 122884
  112.7 6.2 %collective-permute-start.9 = (f32[80,128]{1,0:T(8,128)S(1)}, f32[80,128]{1,0:T(8,128)S(1)}, u32[]{:S(2)}, u32[]{:S(2)}) collective-permute-start(f32[80,128]{1,0:T(8,128)S(1)} %fusion), channel_id=1, source_target_pairs={{0,1},{1,0},{2,3},{3,2},{4,5},{5,4},{6,7},{7,6},{8,9},{9,8},{10,11... | collective-permute-start | bytes 122888 | tf_op jit(solution)/shard_map/ppermute | solution.py:170
  118.9 12.9 %collective-permute-start.10 = (f32[80,128]{1,0:T(8,128)S(1)}, f32[80,128]{1,0:T(8,128)S(1)}, u32[]{:S(2)}, u32[]{:S(2)}) collective-permute-start(f32[80,128]{1,0:T(8,128)S(1)} %fusion.3), channel_id=1, source_target_pairs={{0,256},{256,0},{1,257},{257,1},{2,258},{258,2},{3,259},{259,3},{4... | collective-permute-start | bytes 122888 | tf_op jit(solution)/shard_map/ppermute | solution.py:193

commit v2 on v0

v2 whole, which is shorter than its diff:
```python
import functools
import math

import jax
import jax.numpy as jnp
from jax import lax
from jax.experimental import pallas as pl
from jax.experimental.pallas import tpu as pltpu
from jax.sharding import PartitionSpec as P

HEADS = 32
HEAD_DIM = 128
CHANNELS = 64
STEPS = 50
GUIDANCE = 5.0
FLOW_SHIFT = 5.0
EPSILON = 1e-06
VMEM_LIMIT = 24 * 1024 * 1024
PACK_VMEM_LIMIT = 60 * 1024 * 1024


def sigma_at(progress):
    remain = 1.0 - progress / STEPS
    return FLOW_SHIFT * remain / (1.0 + (FLOW_SHIFT - 1.0) * remain)


def params(limit=VMEM_LIMIT):
    return pltpu.CompilerParams(vmem_limit_bytes=limit)


def normed(values, gain):
    values = values.astype(jnp.float32)
    mean_square = jnp.mean(values * values, axis=-1, keepdims=True)
    return (values * lax.rsqrt(mean_square + EPSILON) * gain).astype(jnp.bfloat16)


def mapped_pair(values, map_ref, first):
    columns = map_ref[:, first : first + 2 * HEAD_DIM]
    none = jnp.zeros((CHANNELS, HEAD_DIM), jnp.bfloat16)
    both = jnp.concatenate(
        [
            jnp.concatenate([columns[:, :HEAD_DIM], none], axis=1),
            jnp.concatenate([none, columns[:, HEAD_DIM:]], axis=1),
        ],
        axis=0,
    )
    return lax.dot_general(
        values, both, (((1,), (1,)), ((), ())), preferred_element_type=jnp.float32
    ).astype(jnp.bfloat16)


def pack_kernel(groups, late, pieces, place_ref, *refs):
    outs = 1 if not late else groups
    sources, gains, map_hbm = refs[:3], refs[3:5], refs[5]
    out_refs = refs[6 : 6 + outs]
    held, gain_refs, map_ref, stage, in_sems, small_sems, out_sems = refs[6 + outs :]
    rows, features = sources[0].shape
    width = features // groups
    head_part = width - HEAD_DIM
    step = rows // pieces
    small = [
        pltpu.make_async_copy(gains[0], gain_refs.at[0], small_sems.at[0]),
        pltpu.make_async_copy(gains[1], gain_refs.at[1], small_sems.at[1]),
        pltpu.make_async_copy(map_hbm, map_ref, small_sems.at[2]),
    ]
    loads = [
        [
            pltpu.make_async_copy(
                sources[which].at[pl.ds(piece * step, step)],
                held.at[which, pl.ds(piece * step, step)],
                in_sems.at[which, piece],
            )
            for which in range(3)
        ]
        for piece in range(pieces)
    ]
    for load in loads[0] + small:
        load.start()
    for piece in loads[1:]:
        for load in piece:
            load.start()
    for load in small:
        load.wait()
    place = place_ref[0]
    stores = []
    for piece in range(pieces):
        for load in loads[piece]:
            load.wait()
        at = slice(piece * step, (piece + 1) * step)
        query_normed = normed(held[0, at, :], gain_refs[0])
        key_normed = normed(held[1, at, :], gain_refs[1])
        for group in range(groups):
            start = group * width
            if late:
                first, last = start + head_part, start + width
                pair = start + 2 * HEAD_DIM
            else:
                first, last = start, start + head_part
                pair = start
            size = last - first
            stage[group, at, :size] = query_normed[:, first:last]
            stage[group, at, size : 2 * size] = key_normed[:, first:last]
            stage[group, at, 2 * size :] = mapped_pair(
                held[2, at, pair : pair + 2 * HEAD_DIM], map_ref, pair
            )
        there = pl.ds(piece * step, step)
        if late:
            for e in range(groups):
                store = pltpu.make_async_copy(
                    stage.at[jnp.bitwise_xor(place, e), there], out_refs[e].at[there], out_sems.at[piece, e]
                )
                store.start()
                stores.append(store)
        else:
            store = pltpu.make_async_copy(
                stage.at[:, there], out_refs[0].at[:, there], out_sems.at[piece, 0]
            )
            store.start()
            stores.append(store)
    for store in stores:
        store.wait()


def pack(place, query_rows, key_rows, value_rows, query_gain, key_gain, out_map, groups, late, pieces=2):
    rows, features = query_rows.shape
    heads = features // groups // HEAD_DIM
    packed = 2 * (1 if late else heads - 1) * HEAD_DIM + 2 * CHANNELS
    hbm = pl.BlockSpec(memory_space=pltpu.HBM)
    if late:
        out_shape = [pltpu.HBM((rows, packed), jnp.bfloat16)] * groups
    else:
        out_shape = [pltpu.HBM((groups, rows, packed), jnp.bfloat16)]
    return pl.pallas_call(
        functools.partial(pack_kernel, groups, late, pieces),
        out_shape=out_shape,
        in_specs=[pl.BlockSpec(memory_space=pltpu.SMEM)] + [hbm] * 6,
        out_specs=[hbm] * len(out_shape),
        scratch_shapes=[
            pltpu.VMEM((3, rows, features), jnp.bfloat16),
            pltpu.VMEM((2, 1, features), jnp.float32),
            pltpu.VMEM((CHANNELS, features), jnp.bfloat16),
            pltpu.VMEM((groups, rows, packed), jnp.bfloat16),
            pltpu.SemaphoreType.DMA((3, pieces)),
            pltpu.SemaphoreType.DMA((3,)),
            pltpu.SemaphoreType.DMA((pieces, groups)),
        ],
        compiler_params=params(PACK_VMEM_LIMIT),
        cost_estimate=pl.CostEstimate(flops=2**28, bytes_accessed=8 * 2**20, transcendentals=0),
        name="pack_late" if late else "pack_early",
    )(place, query_rows, key_rows, value_rows, query_gain, key_gain, out_map)


def scores_between(queries, keys):
    return lax.dot_general(
        queries, keys, (((1,), (1,)), ((), ())), preferred_element_type=jnp.float32
    )


def softmax_weights(scores):
    factor = math.log2(math.e) / math.sqrt(HEAD_DIM)
    top = jnp.max(scores, axis=-1, keepdims=True)
    weights = jnp.exp2((scores - top) * factor)
    return (weights * (1.0 / jnp.sum(weights, axis=-1, keepdims=True))).astype(jnp.bfloat16)


def left_half():
    return lax.broadcasted_iota(jnp.int32, (1, 2 * CHANNELS), 1) < CHANNELS


def early_kernel(chunk, data_ref, term_ref, weights_ref):
    heads = 3
    mapped = data_ref[:, 2 * heads * HEAD_DIM :]

    @pl.loop(0, data_ref.shape[0] // chunk)
    def _(index):
        rows = pl.ds(pl.multiple_of(index * chunk, chunk), chunk)
        terms = []
        for head in range(heads):
            lanes = slice(head * HEAD_DIM, (head + 1) * HEAD_DIM)
            keys = slice((heads + head) * HEAD_DIM, (heads + head + 1) * HEAD_DIM)
            weights = softmax_weights(scores_between(data_ref[rows, lanes], data_ref[:, keys]))
            if head < 2:
                terms.append(jnp.dot(weights, mapped, preferred_element_type=jnp.float32))
            else:
                weights_ref[rows, :] = weights
        term_ref[rows, :] = jnp.where(left_half(), terms[0], terms[1])


def late_kernel(chunk, groups, place_ref, term_ref, weights_ref, *refs):
    held_refs, out_ref, data_ref = refs[:groups], refs[groups], refs[groups + 1]
    part = held_refs[0].shape[0]
    place = place_ref[0]
    for e in range(groups):
        first = pl.multiple_of(jnp.bitwise_xor(place, e) * part, part)
        data_ref[pl.ds(first, part), :] = held_refs[e][...]
    half = part // 2
    mapped = data_ref[:, 2 * HEAD_DIM :]
    count = data_ref.shape[0] // chunk

    def scores_of(index):
        return scores_between(
            data_ref[index * chunk : (index + 1) * chunk, :HEAD_DIM], data_ref[:, HEAD_DIM : 2 * HEAD_DIM]
        )

    ahead = scores_of(0)
    for index in range(count):
        scores = ahead
        if index + 1 < count:
            ahead = scores_of(index + 1)
        rows = slice(index * chunk, (index + 1) * chunk)
        second = jnp.dot(weights_ref[rows, :], mapped, preferred_element_type=jnp.float32)
        third = jnp.dot(softmax_weights(scores), mapped, preferred_element_type=jnp.float32)
        total = term_ref[rows, :] + jnp.where(left_half(), second, third)
        total = total + pltpu.roll(total, CHANNELS, 1)
        for block in range(chunk // part):
            first = block * part
            out_ref[index * (chunk // part) + block] = jnp.where(
                left_half(), total[first : first + half], total[first + half : first + part]
            )


def attend_early(data, chunk=320):
    keys = data.shape[0]
    vmem = pl.BlockSpec(memory_space=pltpu.VMEM)
    return pl.pallas_call(
        functools.partial(early_kernel, chunk),
        out_shape=[
            jax.ShapeDtypeStruct((keys, 2 * CHANNELS), jnp.float32),
            jax.ShapeDtypeStruct((keys, keys), jnp.bfloat16),
        ],
        in_specs=[vmem],
        out_specs=[vmem, vmem],
        compiler_params=params(),
        cost_estimate=pl.CostEstimate(
            flops=8 * 10**9, bytes_accessed=2 * data.size, transcendentals=3 * keys * keys
        ),
        name="attend_early",
    )(data)


def attend_late(place, term, weights, held, chunk=320):
    groups = len(held)
    part, width = held[0].shape
    vmem = pl.BlockSpec(memory_space=pltpu.VMEM)
    return pl.pallas_call(
        functools.partial(late_kernel, chunk, groups),
        out_shape=jax.ShapeDtypeStruct((groups, part // 2, 2 * CHANNELS), jnp.float32),
        in_specs=[pl.BlockSpec(memory_space=pltpu.SMEM)] + [vmem] * (groups + 2),
        out_specs=vmem,
        scratch_shapes=[pltpu.VMEM((groups * part, width), jnp.bfloat16)],
        compiler_params=params(),
        cost_estimate=pl.CostEstimate(
            flops=3 * 10**9, bytes_accessed=2 * 10**6, transcendentals=(groups * part) ** 2
        ),
        name="attend_late",
    )(place, term, weights, *held)


def finish_kernel(index_ref, both_ref, latents_ref, next_ref, denoised_ref):
    progress = index_ref[0].astype(jnp.float32)
    sigma_now = sigma_at(progress)
    sigma_next = sigma_at(progress + 1.0)
    turned = (both_ref[0] + both_ref[1]).T
    guided = jnp.concatenate([turned[:CHANNELS], turned[CHANNELS:]], axis=1)
    latents = latents_ref[...]
    next_ref[...] = latents + (sigma_next - sigma_now) * guided
    denoised_ref[...] = latents - sigma_now * guided


def finish(step_index, both, latents):
    vmem = pl.BlockSpec(memory_space=pltpu.VMEM)
    return pl.pallas_call(
        finish_kernel,
        out_shape=[jax.ShapeDtypeStruct(latents.shape, latents.dtype)] * 2,
        in_specs=[pl.BlockSpec(memory_space=pltpu.SMEM), vmem, vmem],
        out_specs=[vmem, vmem],
        compiler_params=params(),
        cost_estimate=pl.CostEstimate(flops=2**16, bytes_accessed=2**17, transcendentals=0),
        name="finish",
    )(step_index, both, latents)


def local(query_rows, key_rows, value_rows, query_gain, key_gain, out_map, latents, step_index):
    groups = lax.axis_size("seq")
    place = lax.axis_index("seq").astype(jnp.int32).reshape(1)
    rows = query_rows.shape[1]
    sources = (
        place,
        query_rows[0],
        key_rows[0],
        value_rows[0],
        query_gain.reshape(1, -1),
        key_gain.reshape(1, -1),
        out_map.T,
        groups,
    )
    (early,) = pack(*sources, False)
    data = lax.all_to_all(early, "seq", split_axis=0, concat_axis=0, tiled=True)
    late = list(pack(*sources, True))
    late[2], late[1], data = lax.optimization_barrier((late[2], late[1], data))
    held = {0: late[0]}
    for e in (4, 5, 6, 7, 3, 2, 1):
        held[e] = lax.ppermute(late[e], "seq", [(i, i ^ e) for i in range(groups)])
    term, weights = attend_early(data.reshape(groups * rows, data.shape[2]))
    terms = attend_late(place, term, weights, [held[e] for e in range(groups)])
    terms = lax.all_to_all(terms, "seq", split_axis=0, concat_axis=0, tiled=True)
    share = jnp.where(lax.axis_index("cfg") == 0, GUIDANCE, 1.0 - GUIDANCE)
    mine = jnp.sum(terms, axis=0) * share
    both = lax.all_gather(mine, "cfg", axis=0)
    next_latents, denoised = finish(step_index, both, latents.T)
    return (next_latents.T, denoised.T)


def solution(mesh):
    placed = (
        P("cfg", ("batch", "seq"), None),
        P("cfg", ("batch", "seq"), None),
        P("cfg", ("batch", "seq"), None),
        P(),
        P(),
        P(),
        P(("batch", "seq"), None),
        P(),
    )
    return jax.shard_map(
        local,
        mesh=mesh,
        in_specs=placed,
        out_specs=(P(("batch", "seq"), None), P(("batch", "seq"), None)),
        check_vma=False,
    )
```

time: 260 us -> 125 us (0.48)
  waiting for transfers between devices: 128 us -> 47.3 us
  matrix products: 28.5 us -> 0 us
  local copies, waits for them, and re-layouts: 25.4 us -> 0.01 us
  Pallas kernels: 0 us -> 20.7 us
  between operations: 15 us -> 1.43 us
  other arithmetic: 6.55 us -> 0.03 us
  blocking collectives: 17.5 us -> 11.7 us
  starting transfers between devices: 37.8 us -> 43 us
    all_to_all x3 -> x2, waiting for transfers between devices: 92.3 us -> 42.9 us  [the longest x1 32.4 us: local(): data = lax.all_to_all(early, 'seq', split_axis=0, concat_axis=0, tiled=True)]
    unnamed x2 -> x0, waiting for transfers between devices: 36 us -> none
    ppermute x0 -> x7, starting transfers between devices: none -> 30.6 us  [local(): held[e] = lax.ppermute(late[e], 'seq', [(i, i ^ e) for i in range(groups)])]
    all_to_all x3 -> x2, starting transfers between devices: 37.8 us -> 12.3 us  [the longest x1 7.11 us: local(): data = lax.all_to_all(early, 'seq', split_axis=0, concat_axis=0, tiled=True)]
    pallas_call x0 -> x5, Pallas kernels: none -> 20.7 us  [the longest x2 8.5 us: pack(): pl.pallas_call(functools.partial(pack_kernel, groups, late, pieces), out_...]
    dot_general x5 -> x0, matrix products: 17.7 us -> none  [the longest x4 17.2 us: one_block(): jnp.einsum('hqk,khd->qhd', weights_bf, value_part, preferred_element_type...]
    psum x1 -> x0, blocking collectives: 17.5 us -> none  [local(): guided = lax.psum(summed, 'cfg')]
    all_gather x0 -> x1, blocking collectives: none -> 11.7 us  [local(): both = lax.all_gather(mine, 'cfg', axis=0)]
  transfers between devices with their start and end apart: 4 -> 9, of which waited for: 4 -> 5; matrix products, arithmetic and copies ran while one was open for 6% -> 0% of each run, Pallas kernels for 0% -> 9%
where the time goes in v2:
time: 125 us; the launch traced here: 124 us
  waiting for transfers between devices  47.3 us (38%)
  starting transfers between devices  43 us (34%)
  Pallas kernels  20.7 us (17%)
  blocking collectives  11.7 us (9%)
  between operations  1.43 us (1%)
    all_to_all x1, waiting for transfers between devices, local(): data = lax.all_to_all(early, 'seq', split_axis=0, concat_axis=0, tiled=True)  32.4 us
    ppermute x7, starting transfers between devices, local(): held[e] = lax.ppermute(late[e], 'seq', [(i, i ^ e) for i in range(groups)])  30.6 us
    all_gather x1, blocking collectives, local(): both = lax.all_gather(mine, 'cfg', axis=0)  11.7 us
    all_to_all x1, waiting for transfers between devices, local(): lax.all_to_all(terms, 'seq', split_axis=0, concat_axis=0, tiled=True)  10.5 us
    pallas_call x2, Pallas kernels, pack(): pl.pallas_call(functools.partial(pack_kernel, groups, late, pieces), out_...  8.5 us
    pallas_call x1, Pallas kernels, attend_early(): pl.pallas_call(functools.partial(early_kernel, chunk), out_shape=[jax.Sha...  7.32 us
    all_to_all x1, starting transfers between devices, local(): data = lax.all_to_all(early, 'seq', split_axis=0, concat_axis=0, tiled=True)  7.11 us
    all_to_all x1, starting transfers between devices, local(): lax.all_to_all(terms, 'seq', split_axis=0, concat_axis=0, tiled=True)  5.23 us
  transfers between devices with their start and end apart: 9, of which 5 were waited for; matrix products, arithmetic and copies ran while one was open for 0% of the time, Pallas kernels for 9%

profile of v2, /device:TPU:6, one launch (start us, length us, event | category | flops | bytes accessed | tf_op | source)
XLA Modules:
  0.0 124.1 jit_solution(10403660798569483253)
XLA Ops:
  0.6 4.5 %pack_early.1 = bf16[8,160,896]{2,1,0:T(8,128)(2,1)} custom-call(s32[1]{0:T(128)} %bitcast.place_ref, bf16[160,4096]{1,0:T(8,128)(2,1)} %bitcast.15, bf16[160,4096]{1,0:T(8,128)(2,1)} %bitcast.17, bf16[160,4096]{1,0:T(8,128)(2,1)} %bitcast.19, f32[1,4096]{1,0:T(1,128)} %bitcast.23, f32[1,4096]{1,0:T(1,128)} %bitcast.25, bf16[64,4096]{1,0:T(8,128)(2,1)} %bitcast.21), custom_call_target="tpu_custom_call" | custom-call | flops 268435456 | bytes 8388608 | tf_op jit(solution)/shard_map/pack_early/pallas_call | solution.py:133
  5.1 7.1 %all-to-all-start = ((bf16[8,160,896]{2,1,0:T(8,128)(2,1)}), bf16[8,160,896]{2,1,0:T(8,128)(2,1)S(1)}, u32[]{:S(2)}, u32[]{:S(2)}) async-start(bf16[8,160,896]{2,1,0:T(8,128)(2,1)} %pack_early.1), calls=%async_computation | async-start | bytes 4587520 | tf_op jit(solution)/shard_map/all_to_all | solution.py:298
  12.2 4.0 %pack_late.1 = (bf16[160,384]{1,0:T(8,128)(2,1)}, bf16[160,384]{1,0:T(8,128)(2,1)}, bf16[160,384]{1,0:T(8,128)(2,1)}, bf16[160,384]{1,0:T(8,128)(2,1)}, bf16[160...) custom-call(s32[1]{0:T(128)} %bitcast.place_ref, ...), custom_call_target="tpu_custom_call" | custom-call | flops 268435456 | bytes 8388608 | tf_op jit(solution)/shard_map/pack_late/pallas_call | solution.py:133
  16.3 5.7 %collective-permute-start.2 = (bf16[160,384]{1,0:T(8,128)(2,1)}, bf16[160,384]{1,0:T(8,128)(2,1)S(1)}, u32[]{:S(2)}, u32[]{:S(2)}) collective-permute-start(bf16[160,384]{1,0:T(8,128)(2,1)} %get-tuple-element.25), channel_id=1, source_target_pairs={{0,3},{1,2},{2,1},{3,0},{4,7},{5,6},{6,5},{7,4},{8,11},{9,10},{10,... | collective-permute-start | bytes 368648 | tf_op jit(solution)/shard_map/ppermute | solution.py:303
  22.0 4.6 %collective-permute-start.3 = (bf16[160,384]{1,0:T(8,128)(2,1)}, bf16[160,384]{1,0:T(8,128)(2,1)S(1)}, u32[]{:S(2)}, u32[]{:S(2)}) collective-permute-start(bf16[160,384]{1,0:T(8,128)(2,1)} %get-tuple-element.26), channel_id=1, source_target_pairs={{0,4},{1,5},{2,6},{3,7},{4,0},{5,1},{6,2},{7,3},{8,12},{9,13},{10,... | collective-permute-start | bytes 368648 | tf_op jit(solution)/shard_map/ppermute | solution.py:303
  26.6 3.4 %collective-permute-start.4 = (bf16[160,384]{1,0:T(8,128)(2,1)}, bf16[160,384]{1,0:T(8,128)(2,1)S(1)}, u32[]{:S(2)}, u32[]{:S(2)}) collective-permute-start(bf16[160,384]{1,0:T(8,128)(2,1)} %get-tuple-element.27), channel_id=1, source_target_pairs={{0,5},{1,4},{2,7},{3,6},{4,1},{5,0},{6,3},{7,2},{8,13},{9,12},{10,... | collective-permute-start | bytes 368648 | tf_op jit(solution)/shard_map/ppermute | solution.py:303
  30.0 6.4 %collective-permute-start.5 = (bf16[160,384]{1,0:T(8,128)(2,1)}, bf16[160,384]{1,0:T(8,128)(2,1)S(1)}, u32[]{:S(2)}, u32[]{:S(2)}) collective-permute-start(bf16[160,384]{1,0:T(8,128)(2,1)} %get-tuple-element.28), channel_id=1, source_target_pairs={{0,6},{1,7},{2,4},{3,5},{4,2},{5,3},{6,0},{7,1},{8,14},{9,15},{10,... | collective-permute-start | bytes 368648 | tf_op jit(solution)/shard_map/ppermute | solution.py:303
  36.4 2.5 %collective-permute-start.6 = (bf16[160,384]{1,0:T(8,128)(2,1)}, bf16[160,384]{1,0:T(8,128)(2,1)S(1)}, u32[]{:S(2)}, u32[]{:S(2)}) collective-permute-start(bf16[160,384]{1,0:T(8,128)(2,1)} %get-tuple-element.29), channel_id=1, source_target_pairs={{0,7},{1,6},{2,5},{3,4},{4,3},{5,2},{6,1},{7,0},{8,15},{9,14},{10,... | collective-permute-start | bytes 368648 | tf_op jit(solution)/shard_map/ppermute | solution.py:303
  38.8 32.4 %all-to-all-done = bf16[8,160,896]{2,1,0:T(8,128)(2,1)S(1)} async-done(((bf16[8,160,896]{2,1,0:T(8,128)(2,1)}), bf16[8,160,896]{2,1,0:T(8,128)(2,1)S(1)}, u32[]{:S(2)}, u32[]{:S(2)}) %all-to-all-start) | async-done | bytes 2293792 | tf_op jit(solution)/shard_map/all_to_all | solution.py:298
  71.2 3.2 %collective-permute-done.2.refs_3_ = bf16[160,384]{1,0:T(8,128)(2,1)S(1)} collective-permute-done((bf16[160,384]{1,0:T(8,128)(2,1)}, bf16[160,384]{1,0:T(8,128)(2,1)S(1)}, u32[]{:S(2)}, u32[]{:S(2)}) %collective-permute-start.2) | collective-permute-done | bytes 122912 | tf_op jit(solution)/shard_map/ppermute | solution.py:303
  74.5 6.2 %collective-permute-start = (bf16[160,384]{1,0:T(8,128)(2,1)}, bf16[160,384]{1,0:T(8,128)(2,1)S(1)}, u32[]{:S(2)}, u32[]{:S(2)}) collective-permute-start(bf16[160,384]{1,0:T(8,128)(2,1)} %get-tuple-element.23), channel_id=1, source_target_pairs={{0,1},{1,0},{2,3},{3,2},{4,5},{5,4},{6,7},{7,6},{8,9},{9,8},{10,11... | collective-permute-start | bytes 368648 | tf_op jit(solution)/shard_map/ppermute | solution.py:303
  80.7 0.1 collective-permute-done.3.refs_4_
  80.7 1.9 %collective-permute-start.1 = (bf16[160,384]{1,0:T(8,128)(2,1)}, bf16[160,384]{1,0:T(8,128)(2,1)S(1)}, u32[]{:S(2)}, u32[]{:S(2)}) collective-permute-start(bf16[160,384]{1,0:T(8,128)(2,1)} %get-tuple-element.24), channel_id=1, source_target_pairs={{0,2},{1,3},{2,0},{3,1},{4,6},{5,7},{6,4},{7,5},{8,10},{9,11},{10,... | collective-permute-start | bytes 368648 | tf_op jit(solution)/shard_map/ppermute | solution.py:303
  82.7 7.3 %attend_early.1 = (f32[1280,128]{1,0:T(8,128)S(1)}, bf16[1280,1280]{1,0:T(8,128)(2,1)S(1)}) custom-call(bf16[1280,896]{1,0:T(8,128)(2,1)S(1)} %bitcast.12), custom_call_target="tpu_custom_call" | custom-call | flops 8000000000 | bytes 2293760 | tf_op jit(solution)/shard_map/attend_early/pallas_call | solution.py:225
  90.0 0.0 collective-permute-done.4.refs_5_
  90.0 0.0 collective-permute-done.5.refs_6_
  90.0 0.0 collective-permute-done.6.refs_7_
  90.0 0.0 collective-permute-done.refs_1_
  90.0 1.1 collective-permute-done.1.refs_2_
  91.1 4.0 %attend_late.1 = f32[8,80,128]{2,1,0:T(8,128)} custom-call(s32[1]{0:T(128)} %bitcast.place_ref, f32[1280,128]{1,0:T(8,128)S(1)} %get-tuple-element.20.term_ref, bf16[1280,1280]{1,0:T(8,128)(2,1)S(1)} %get-tuple-element.21.weights_ref, bf16[160,384]{1,0:T(8,128)(2,1)S(1)} %copy-done.1, bf16[160,384]{1,0:T(8,128)(2,1)S(1)} %collective-permute-done.refs_1_, ...), custom_call_target="tpu_custom_call" | custom-call | flops 3000000000 | bytes 2000000 | tf_op jit(solution)/shard_map/attend_late/pallas_call | solution.py:245
  95.1 5.2 %all-to-all-start.1 = ((f32[8,80,128]{2,1,0:T(8,128)}), f32[8,80,128]{2,1,0:T(8,128)S(1)}, u32[]{:S(2)}, u32[]{:S(2)}) async-start(f32[8,80,128]{2,1,0:T(8,128)} %attend_late.1), calls=%async_computation.1 | async-start | bytes 655360 | tf_op jit(solution)/shard_map/all_to_all | solution.py:306
  101.0 10.5 %all-to-all-done.1 = f32[8,80,128]{2,1,0:T(8,128)S(1)} async-done(((f32[8,80,128]{2,1,0:T(8,128)}), f32[8,80,128]{2,1,0:T(8,128)S(1)}, u32[]{:S(2)}, u32[]{:S(2)}) %all-to-all-start.1) | async-done | bytes 327712 | tf_op jit(solution)/shard_map/all_to_all | solution.py:306
  111.6 11.7 %all-gather = f32[160,128]{1,0:T(8,128)S(1)} all-gather(f32[80,128]{1,0:T(8,128)S(1)} %broadcast_multiply_fusion), channel_id=2, replica_groups=mesh['cfg'=2,'batch'=32,'seq'=8] {'cfg'}, dimensions={0}, use_global_device_ids=true | all-gather | bytes 122880 | tf_op jit(solution)/shard_map/all_gather | solution.py:309
  123.3 0.8 finish.1
  (6 shorter events, 0.0 us)
Async XLA Ops:
  5.1 66.1 %all-to-all-start = ((bf16[8,160,896]{2,1,0:T(8,128)(2,1)}), bf16[8,160,896]{2,1,0:T(8,128)(2,1)S(1)}, u32[]{:S(2)}, u32[]{:S(2)}) async-start(bf16[8,160,896]{2,1,0:T(8,128)(2,1)} %pack_early.1), calls=%async_computation | async-start | bytes 4587520 | tf_op jit(solution)/shard_map/all_to_all | solution.py:298
  16.3 58.2 %collective-permute-start.2 = (bf16[160,384]{1,0:T(8,128)(2,1)}, bf16[160,384]{1,0:T(8,128)(2,1)S(1)}, u32[]{:S(2)}, u32[]{:S(2)}) collective-permute-start(bf16[160,384]{1,0:T(8,128)(2,1)} %get-tuple-element.25), channel_id=1, source_target_pairs={{0,3},{1,2},{2,1},{3,0},{4,7},{5,6},{6,5},{7,4},{8,11},{9,10},{10,... | collective-permute-start | bytes 368648 | tf_op jit(solution)/shard_map/ppermute | solution.py:303
  22.0 58.7 %collective-permute-start.3 = (bf16[160,384]{1,0:T(8,128)(2,1)}, bf16[160,384]{1,0:T(8,128)(2,1)S(1)}, u32[]{:S(2)}, u32[]{:S(2)}) collective-permute-start(bf16[160,384]{1,0:T(8,128)(2,1)} %get-tuple-element.26), channel_id=1, source_target_pairs={{0,4},{1,5},{2,6},{3,7},{4,0},{5,1},{6,2},{7,3},{8,12},{9,13},{10,... | collective-permute-start | bytes 368648 | tf_op jit(solution)/shard_map/ppermute | solution.py:303
  26.6 63.4 %collective-permute-start.4 = (bf16[160,384]{1,0:T(8,128)(2,1)}, bf16[160,384]{1,0:T(8,128)(2,1)S(1)}, u32[]{:S(2)}, u32[]{:S(2)}) collective-permute-start(bf16[160,384]{1,0:T(8,128)(2,1)} %get-tuple-element.27), channel_id=1, source_target_pairs={{0,5},{1,4},{2,7},{3,6},{4,1},{5,0},{6,3},{7,2},{8,13},{9,12},{10,... | collective-permute-start | bytes 368648 | tf_op jit(solution)/shard_map/ppermute | solution.py:303
  30.0 60.0 %collective-permute-start.5 = (bf16[160,384]{1,0:T(8,128)(2,1)}, bf16[160,384]{1,0:T(8,128)(2,1)S(1)}, u32[]{:S(2)}, u32[]{:S(2)}) collective-permute-start(bf16[160,384]{1,0:T(8,128)(2,1)} %get-tuple-element.28), channel_id=1, source_target_pairs={{0,6},{1,7},{2,4},{3,5},{4,2},{5,3},{6,0},{7,1},{8,14},{9,15},{10,... | collective-permute-start | bytes 368648 | tf_op jit(solution)/shard_map/ppermute | solution.py:303
  36.4 53.7 %collective-permute-start.6 = (bf16[160,384]{1,0:T(8,128)(2,1)}, bf16[160,384]{1,0:T(8,128)(2,1)S(1)}, u32[]{:S(2)}, u32[]{:S(2)}) collective-permute-start(bf16[160,384]{1,0:T(8,128)(2,1)} %get-tuple-element.29), channel_id=1, source_target_pairs={{0,7},{1,6},{2,5},{3,4},{4,3},{5,2},{6,1},{7,0},{8,15},{9,14},{10,... | collective-permute-start | bytes 368648 | tf_op jit(solution)/shard_map/ppermute | solution.py:303
  74.5 15.6 %collective-permute-start = (bf16[160,384]{1,0:T(8,128)(2,1)}, bf16[160,384]{1,0:T(8,128)(2,1)S(1)}, u32[]{:S(2)}, u32[]{:S(2)}) collective-permute-start(bf16[160,384]{1,0:T(8,128)(2,1)} %get-tuple-element.23), channel_id=1, source_target_pairs={{0,1},{1,0},{2,3},{3,2},{4,5},{5,4},{6,7},{7,6},{8,9},{9,8},{10,11... | collective-permute-start | bytes 368648 | tf_op jit(solution)/shard_map/ppermute | solution.py:303
  80.7 10.3 %collective-permute-start.1 = (bf16[160,384]{1,0:T(8,128)(2,1)}, bf16[160,384]{1,0:T(8,128)(2,1)S(1)}, u32[]{:S(2)}, u32[]{:S(2)}) collective-permute-start(bf16[160,384]{1,0:T(8,128)(2,1)} %get-tuple-element.24), channel_id=1, source_target_pairs={{0,2},{1,3},{2,0},{3,1},{4,6},{5,7},{6,4},{7,5},{8,10},{9,11},{10,... | collective-permute-start | bytes 368648 | tf_op jit(solution)/shard_map/ppermute | solution.py:303
  82.7 8.4 %copy-start.1 = (bf16[160,384]{1,0:T(8,128)(2,1)S(1)}, bf16[160,384]{1,0:T(8,128)(2,1)}, u32[]{:S(2)}) copy-start(bf16[160,384]{1,0:T(8,128)(2,1)} %get-tuple-element.22.refs_0_) | copy-start | bytes 368644
  91.1 32.2 %copy-start = (f32[160,64]{0,1:T(8,128)S(1)}, f32[160,64]{0,1:T(8,128)}, u32[]{:S(2)}) copy-start(f32[160,64]{0,1:T(8,128)} %param.14) | copy-start | bytes 122884
  95.1 16.4 %all-to-all-start.1 = ((f32[8,80,128]{2,1,0:T(8,128)}), f32[8,80,128]{2,1,0:T(8,128)S(1)}, u32[]{:S(2)}, u32[]{:S(2)}) async-start(f32[8,80,128]{2,1,0:T(8,128)} %attend_late.1), calls=%async_computation.1 | async-start | bytes 655360 | tf_op jit(solution)/shard_map/all_to_all | solution.py:306

commit v3 on v2

--- a/solution.py
+++ b/solution.py
@@ -17,6 +17,7 @@
 EPSILON = 1e-06
 VMEM_LIMIT = 24 * 1024 * 1024
 PACK_VMEM_LIMIT = 60 * 1024 * 1024
+PIECES = 2
 
 
 def sigma_at(progress):
@@ -49,7 +50,7 @@
     ).astype(jnp.bfloat16)
 
 
-def pack_kernel(groups, late, pieces, place_ref, *refs):
+def pack_kernel(groups, late, cuts, place_ref, *refs):
     outs = 1 if not late else groups
     sources, gains, map_hbm = refs[:3], refs[3:5], refs[5]
     out_refs = refs[6 : 6 + outs]
@@ -57,7 +58,7 @@
     rows, features = sources[0].shape
     width = features // groups
     head_part = width - HEAD_DIM
-    step = rows // pieces
+    pieces = len(cuts) - 1
     small = [
         pltpu.make_async_copy(gains[0], gain_refs.at[0], small_sems.at[0]),
         pltpu.make_async_copy(gains[1], gain_refs.at[1], small_sems.at[1]),
@@ -66,8 +67,8 @@
     loads = [
         [
             pltpu.make_async_copy(
-                sources[which].at[pl.ds(piece * step, step)],
-                held.at[which, pl.ds(piece * step, step)],
+                sources[which].at[pl.ds(cuts[piece], cuts[piece + 1] - cuts[piece])],
+                held.at[which, pl.ds(cuts[piece], cuts[piece + 1] - cuts[piece])],
                 in_sems.at[which, piece],
             )
             for which in range(3)
@@ -86,7 +87,7 @@
     for piece in range(pieces):
         for load in loads[piece]:
             load.wait()
-        at = slice(piece * step, (piece + 1) * step)
+        at = slice(cuts[piece], cuts[piece + 1])
         query_normed = normed(held[0, at, :], gain_refs[0])
         key_normed = normed(held[1, at, :], gain_refs[1])
         for group in range(groups):
@@ -103,7 +104,7 @@
             stage[group, at, 2 * size :] = mapped_pair(
                 held[2, at, pair : pair + 2 * HEAD_DIM], map_ref, pair
             )
-        there = pl.ds(piece * step, step)
+        there = pl.ds(cuts[piece], cuts[piece + 1] - cuts[piece])
         if late:
             for e in range(groups):
                 store = pltpu.make_async_copy(
@@ -121,8 +122,10 @@
         store.wait()
 
 
-def pack(place, query_rows, key_rows, value_rows, query_gain, key_gain, out_map, groups, late, pieces=2):
+def pack(place, query_rows, key_rows, value_rows, query_gain, key_gain, out_map, groups, late):
     rows, features = query_rows.shape
+    cuts = [rows // 16 * part // PIECES * 16 for part in range(PIECES)] + [rows]
+    pieces = len(cuts) - 1
     heads = features // groups // HEAD_DIM
     packed = 2 * (1 if late else heads - 1) * HEAD_DIM + 2 * CHANNELS
     hbm = pl.BlockSpec(memory_space=pltpu.HBM)
@@ -131,7 +134,7 @@
     else:
         out_shape = [pltpu.HBM((groups, rows, packed), jnp.bfloat16)]
     return pl.pallas_call(
-        functools.partial(pack_kernel, groups, late, pieces),
+        functools.partial(pack_kernel, groups, late, cuts),
         out_shape=out_shape,
         in_specs=[pl.BlockSpec(memory_space=pltpu.SMEM)] + [hbm] * 6,
         out_specs=[hbm] * len(out_shape),
@@ -297,9 +300,9 @@
     (early,) = pack(*sources, False)
     data = lax.all_to_all(early, "seq", split_axis=0, concat_axis=0, tiled=True)
     late = list(pack(*sources, True))
-    late[2], late[1], data = lax.optimization_barrier((late[2], late[1], data))
+    late[3], late[2], data = lax.optimization_barrier((late[3], late[2], data))
     held = {0: late[0]}
-    for e in (4, 5, 6, 7, 3, 2, 1):
+    for e in (1, 4, 5, 6, 7, 2, 3):
         held[e] = lax.ppermute(late[e], "seq", [(i, i ^ e) for i in range(groups)])
     term, weights = attend_early(data.reshape(groups * rows, data.shape[2]))
     terms = attend_late(place, term, weights, [held[e] for e in range(groups)])

time: 125 us -> 122 us (0.976)
  starting transfers between devices: 43 us -> 36.5 us
  waiting for transfers between devices: 47.3 us -> 51.3 us
    ppermute x7, starting transfers between devices: 30.6 us -> 25.3 us  [local(): held[e] = lax.ppermute(late[e], 'seq', [(i, i ^ e) for i in range(groups)])]
    ppermute x7, waiting for transfers between devices: 4.4 us -> 8.53 us  [local(): held[e] = lax.ppermute(late[e], 'seq', [(i, i ^ e) for i in range(groups)])]
where the time goes in v3:
time: 122 us
  waiting for transfers between devices  51.3 us (42%)
  starting transfers between devices  36.5 us (30%)
  Pallas kernels  20.7 us (17%)
  blocking collectives  11.7 us (10%)
  between operations  1.43 us (1%)
    all_to_all x1, waiting for transfers between devices, local(): data = lax.all_to_all(early, 'seq', split_axis=0, concat_axis=0, tiled=True)  31.3 us
    ppermute x7, starting transfers between devices, local(): held[e] = lax.ppermute(late[e], 'seq', [(i, i ^ e) for i in range(groups)])  25.3 us
    all_gather x1, blocking collectives, local(): both = lax.all_gather(mine, 'cfg', axis=0)  11.7 us
    all_to_all x1, waiting for transfers between devices, local(): lax.all_to_all(terms, 'seq', split_axis=0, concat_axis=0, tiled=True)  11.5 us
    ppermute x7, waiting for transfers between devices, local(): held[e] = lax.ppermute(late[e], 'seq', [(i, i ^ e) for i in range(groups)])  8.53 us
    pallas_call x2, Pallas kernels, pack(): pl.pallas_call(functools.partial(pack_kernel, groups, late, cuts), out_sh...  8.5 us
    pallas_call x1, Pallas kernels, attend_early(): pl.pallas_call(functools.partial(early_kernel, chunk), out_shape=[jax.Sha...  7.32 us
    all_to_all x1, starting transfers between devices, local(): data = lax.all_to_all(early, 'seq', split_axis=0, concat_axis=0, tiled=True)  7.11 us
  transfers between devices with their start and end apart: 9, of which 5 were waited for; matrix products, arithmetic and copies ran while one was open for 0% of the time, Pallas kernels for 9%

profile of v3, /device:TPU:6, one launch (start us, length us, event | category | flops | bytes accessed | tf_op | source)
XLA Modules:
  0.0 121.6 jit_solution(1857185870077051530)
XLA Ops:
  0.6 4.5 %pack_early.1 = bf16[8,160,896]{2,1,0:T(8,128)(2,1)} custom-call(s32[1]{0:T(128)} %bitcast.place_ref, bf16[160,4096]{1,0:T(8,128)(2,1)} %bitcast.15, bf16[160,4096]{1,0:T(8,128)(2,1)} %bitcast.17, bf16[160,4096]{1,0:T(8,128)(2,1)} %bitcast.19, f32[1,4096]{1,0:T(1,128)} %bitcast.23, f32[1,4096]{1,0:T(1,128)} %bitcast.25, bf16[64,4096]{1,0:T(8,128)(2,1)} %bitcast.21), custom_call_target="tpu_custom_call" | custom-call | flops 268435456 | bytes 8388608 | tf_op jit(solution)/shard_map/pack_early/pallas_call | solution.py:136
  5.1 7.1 %all-to-all-start = ((bf16[8,160,896]{2,1,0:T(8,128)(2,1)}), bf16[8,160,896]{2,1,0:T(8,128)(2,1)S(1)}, u32[]{:S(2)}, u32[]{:S(2)}) async-start(bf16[8,160,896]{2,1,0:T(8,128)(2,1)} %pack_early.1), calls=%async_computation | async-start | bytes 4587520 | tf_op jit(solution)/shard_map/all_to_all | solution.py:301
  12.2 4.0 %pack_late.1 = (bf16[160,384]{1,0:T(8,128)(2,1)}, bf16[160,384]{1,0:T(8,128)(2,1)}, bf16[160,384]{1,0:T(8,128)(2,1)}, bf16[160,384]{1,0:T(8,128)(2,1)}, bf16[160...) custom-call(s32[1]{0:T(128)} %bitcast.place_ref, ...), custom_call_target="tpu_custom_call" | custom-call | flops 268435456 | bytes 8388608 | tf_op jit(solution)/shard_map/pack_late/pallas_call | solution.py:136
  16.3 3.9 %collective-permute-start = (bf16[160,384]{1,0:T(8,128)(2,1)}, bf16[160,384]{1,0:T(8,128)(2,1)S(1)}, u32[]{:S(2)}, u32[]{:S(2)}) collective-permute-start(bf16[160,384]{1,0:T(8,128)(2,1)} %get-tuple-element.23), channel_id=1, source_target_pairs={{0,1},{1,0},{2,3},{3,2},{4,5},{5,4},{6,7},{7,6},{8,9},{9,8},{10,11... | collective-permute-start | bytes 368648 | tf_op jit(solution)/shard_map/ppermute | solution.py:306
  20.2 6.4 %collective-permute-start.3 = (bf16[160,384]{1,0:T(8,128)(2,1)}, bf16[160,384]{1,0:T(8,128)(2,1)S(1)}, u32[]{:S(2)}, u32[]{:S(2)}) collective-permute-start(bf16[160,384]{1,0:T(8,128)(2,1)} %get-tuple-element.26), channel_id=1, source_target_pairs={{0,4},{1,5},{2,6},{3,7},{4,0},{5,1},{6,2},{7,3},{8,12},{9,13},{10,... | collective-permute-start | bytes 368648 | tf_op jit(solution)/shard_map/ppermute | solution.py:306
  26.6 1.9 %collective-permute-start.4 = (bf16[160,384]{1,0:T(8,128)(2,1)}, bf16[160,384]{1,0:T(8,128)(2,1)S(1)}, u32[]{:S(2)}, u32[]{:S(2)}) collective-permute-start(bf16[160,384]{1,0:T(8,128)(2,1)} %get-tuple-element.27), channel_id=1, source_target_pairs={{0,5},{1,4},{2,7},{3,6},{4,1},{5,0},{6,3},{7,2},{8,13},{9,12},{10,... | collective-permute-start | bytes 368648 | tf_op jit(solution)/shard_map/ppermute | solution.py:306
  28.5 6.0 %collective-permute-start.5 = (bf16[160,384]{1,0:T(8,128)(2,1)}, bf16[160,384]{1,0:T(8,128)(2,1)S(1)}, u32[]{:S(2)}, u32[]{:S(2)}) collective-permute-start(bf16[160,384]{1,0:T(8,128)(2,1)} %get-tuple-element.28), channel_id=1, source_target_pairs={{0,6},{1,7},{2,4},{3,5},{4,2},{5,3},{6,0},{7,1},{8,14},{9,15},{10,... | collective-permute-start | bytes 368648 | tf_op jit(solution)/shard_map/ppermute | solution.py:306
  34.6 2.5 %collective-permute-start.6 = (bf16[160,384]{1,0:T(8,128)(2,1)}, bf16[160,384]{1,0:T(8,128)(2,1)S(1)}, u32[]{:S(2)}, u32[]{:S(2)}) collective-permute-start(bf16[160,384]{1,0:T(8,128)(2,1)} %get-tuple-element.29), channel_id=1, source_target_pairs={{0,7},{1,6},{2,5},{3,4},{4,3},{5,2},{6,1},{7,0},{8,15},{9,14},{10,... | collective-permute-start | bytes 368648 | tf_op jit(solution)/shard_map/ppermute | solution.py:306
  37.0 31.3 %all-to-all-done = bf16[8,160,896]{2,1,0:T(8,128)(2,1)S(1)} async-done(((bf16[8,160,896]{2,1,0:T(8,128)(2,1)}), bf16[8,160,896]{2,1,0:T(8,128)(2,1)S(1)}, u32[]{:S(2)}, u32[]{:S(2)}) %all-to-all-start) | async-done | bytes 2293792 | tf_op jit(solution)/shard_map/all_to_all | solution.py:301
  68.3 4.8 %collective-permute-done.refs_1_ = bf16[160,384]{1,0:T(8,128)(2,1)S(1)} collective-permute-done((bf16[160,384]{1,0:T(8,128)(2,1)}, bf16[160,384]{1,0:T(8,128)(2,1)S(1)}, u32[]{:S(2)}, u32[]{:S(2)}) %collective-permute-start) | collective-permute-done | bytes 122912 | tf_op jit(solution)/shard_map/ppermute | solution.py:306
  73.1 1.9 %collective-permute-start.1 = (bf16[160,384]{1,0:T(8,128)(2,1)}, bf16[160,384]{1,0:T(8,128)(2,1)S(1)}, u32[]{:S(2)}, u32[]{:S(2)}) collective-permute-start(bf16[160,384]{1,0:T(8,128)(2,1)} %get-tuple-element.24), channel_id=1, source_target_pairs={{0,2},{1,3},{2,0},{3,1},{4,6},{5,7},{6,4},{7,5},{8,10},{9,11},{10,... | collective-permute-start | bytes 368648 | tf_op jit(solution)/shard_map/ppermute | solution.py:306
  75.0 3.0 %collective-permute-done.3.refs_4_ = bf16[160,384]{1,0:T(8,128)(2,1)S(1)} collective-permute-done((bf16[160,384]{1,0:T(8,128)(2,1)}, bf16[160,384]{1,0:T(8,128)(2,1)S(1)}, u32[]{:S(2)}, u32[]{:S(2)}) %collective-permute-start.3) | collective-permute-done | bytes 122912 | tf_op jit(solution)/shard_map/ppermute | solution.py:306
  78.0 2.6 %collective-permute-start.2 = (bf16[160,384]{1,0:T(8,128)(2,1)}, bf16[160,384]{1,0:T(8,128)(2,1)S(1)}, u32[]{:S(2)}, u32[]{:S(2)}) collective-permute-start(bf16[160,384]{1,0:T(8,128)(2,1)} %get-tuple-element.25), channel_id=1, source_target_pairs={{0,3},{1,2},{2,1},{3,0},{4,7},{5,6},{6,5},{7,4},{8,11},{9,10},{10,... | collective-permute-start | bytes 368648 | tf_op jit(solution)/shard_map/ppermute | solution.py:306
  80.7 7.3 %attend_early.1 = (f32[1280,128]{1,0:T(8,128)S(1)}, bf16[1280,1280]{1,0:T(8,128)(2,1)S(1)}) custom-call(bf16[1280,896]{1,0:T(8,128)(2,1)S(1)} %bitcast.12), custom_call_target="tpu_custom_call" | custom-call | flops 8000000000 | bytes 2293760 | tf_op jit(solution)/shard_map/attend_early/pallas_call | solution.py:228
  88.0 0.0 collective-permute-done.4.refs_5_
  88.0 0.0 collective-permute-done.5.refs_6_
  88.0 0.0 collective-permute-done.6.refs_7_
  88.0 0.0 collective-permute-done.1.refs_2_
  88.1 0.7 collective-permute-done.2.refs_3_
  88.8 4.0 %attend_late.1 = f32[8,80,128]{2,1,0:T(8,128)} custom-call(s32[1]{0:T(128)} %bitcast.place_ref, f32[1280,128]{1,0:T(8,128)S(1)} %get-tuple-element.20.term_ref, bf16[1280,1280]{1,0:T(8,128)(2,1)S(1)} %get-tuple-element.21.weights_ref, bf16[160,384]{1,0:T(8,128)(2,1)S(1)} %copy-done.1, bf16[160,384]{1,0:T(8,128)(2,1)S(1)} %collective-permute-done.refs_1_, ...), custom_call_target="tpu_custom_call" | custom-call | flops 3000000000 | bytes 2000000 | tf_op jit(solution)/shard_map/attend_late/pallas_call | solution.py:248
  92.8 4.1 %all-to-all-start.1 = ((f32[8,80,128]{2,1,0:T(8,128)}), f32[8,80,128]{2,1,0:T(8,128)S(1)}, u32[]{:S(2)}, u32[]{:S(2)}) async-start(f32[8,80,128]{2,1,0:T(8,128)} %attend_late.1), calls=%async_computation.1 | async-start | bytes 655360 | tf_op jit(solution)/shard_map/all_to_all | solution.py:309
  97.5 11.5 %all-to-all-done.1 = f32[8,80,128]{2,1,0:T(8,128)S(1)} async-done(((f32[8,80,128]{2,1,0:T(8,128)}), f32[8,80,128]{2,1,0:T(8,128)S(1)}, u32[]{:S(2)}, u32[]{:S(2)}) %all-to-all-start.1) | async-done | bytes 327712 | tf_op jit(solution)/shard_map/all_to_all | solution.py:309
  109.0 11.7 %all-gather = f32[160,128]{1,0:T(8,128)S(1)} all-gather(f32[80,128]{1,0:T(8,128)S(1)} %broadcast_multiply_fusion), channel_id=2, replica_groups=mesh['cfg'=2,'batch'=32,'seq'=8] {'cfg'}, dimensions={0}, use_global_device_ids=true | all-gather | bytes 122880 | tf_op jit(solution)/shard_map/all_gather | solution.py:312
  120.8 0.8 finish.1
  (6 shorter events, 0.0 us)
Async XLA Ops:
  5.1 63.2 %all-to-all-start = ((bf16[8,160,896]{2,1,0:T(8,128)(2,1)}), bf16[8,160,896]{2,1,0:T(8,128)(2,1)S(1)}, u32[]{:S(2)}, u32[]{:S(2)}) async-start(bf16[8,160,896]{2,1,0:T(8,128)(2,1)} %pack_early.1), calls=%async_computation | async-start | bytes 4587520 | tf_op jit(solution)/shard_map/all_to_all | solution.py:301
  16.3 56.8 %collective-permute-start = (bf16[160,384]{1,0:T(8,128)(2,1)}, bf16[160,384]{1,0:T(8,128)(2,1)S(1)}, u32[]{:S(2)}, u32[]{:S(2)}) collective-permute-start(bf16[160,384]{1,0:T(8,128)(2,1)} %get-tuple-element.23), channel_id=1, source_target_pairs={{0,1},{1,0},{2,3},{3,2},{4,5},{5,4},{6,7},{7,6},{8,9},{9,8},{10,11... | collective-permute-start | bytes 368648 | tf_op jit(solution)/shard_map/ppermute | solution.py:306
  20.2 57.8 %collective-permute-start.3 = (bf16[160,384]{1,0:T(8,128)(2,1)}, bf16[160,384]{1,0:T(8,128)(2,1)S(1)}, u32[]{:S(2)}, u32[]{:S(2)}) collective-permute-start(bf16[160,384]{1,0:T(8,128)(2,1)} %get-tuple-element.26), channel_id=1, source_target_pairs={{0,4},{1,5},{2,6},{3,7},{4,0},{5,1},{6,2},{7,3},{8,12},{9,13},{10,... | collective-permute-start | bytes 368648 | tf_op jit(solution)/shard_map/ppermute | solution.py:306
  26.6 61.4 %collective-permute-start.4 = (bf16[160,384]{1,0:T(8,128)(2,1)}, bf16[160,384]{1,0:T(8,128)(2,1)S(1)}, u32[]{:S(2)}, u32[]{:S(2)}) collective-permute-start(bf16[160,384]{1,0:T(8,128)(2,1)} %get-tuple-element.27), channel_id=1, source_target_pairs={{0,5},{1,4},{2,7},{3,6},{4,1},{5,0},{6,3},{7,2},{8,13},{9,12},{10,... | collective-permute-start | bytes 368648 | tf_op jit(solution)/shard_map/ppermute | solution.py:306
  28.5 59.5 %collective-permute-start.5 = (bf16[160,384]{1,0:T(8,128)(2,1)}, bf16[160,384]{1,0:T(8,128)(2,1)S(1)}, u32[]{:S(2)}, u32[]{:S(2)}) collective-permute-start(bf16[160,384]{1,0:T(8,128)(2,1)} %get-tuple-element.28), channel_id=1, source_target_pairs={{0,6},{1,7},{2,4},{3,5},{4,2},{5,3},{6,0},{7,1},{8,14},{9,15},{10,... | collective-permute-start | bytes 368648 | tf_op jit(solution)/shard_map/ppermute | solution.py:306
  34.6 53.5 %collective-permute-start.6 = (bf16[160,384]{1,0:T(8,128)(2,1)}, bf16[160,384]{1,0:T(8,128)(2,1)S(1)}, u32[]{:S(2)}, u32[]{:S(2)}) collective-permute-start(bf16[160,384]{1,0:T(8,128)(2,1)} %get-tuple-element.29), channel_id=1, source_target_pairs={{0,7},{1,6},{2,5},{3,4},{4,3},{5,2},{6,1},{7,0},{8,15},{9,14},{10,... | collective-permute-start | bytes 368648 | tf_op jit(solution)/shard_map/ppermute | solution.py:306
  73.1 15.0 %collective-permute-start.1 = (bf16[160,384]{1,0:T(8,128)(2,1)}, bf16[160,384]{1,0:T(8,128)(2,1)S(1)}, u32[]{:S(2)}, u32[]{:S(2)}) collective-permute-start(bf16[160,384]{1,0:T(8,128)(2,1)} %get-tuple-element.24), channel_id=1, source_target_pairs={{0,2},{1,3},{2,0},{3,1},{4,6},{5,7},{6,4},{7,5},{8,10},{9,11},{10,... | collective-permute-start | bytes 368648 | tf_op jit(solution)/shard_map/ppermute | solution.py:306
  78.0 10.7 %collective-permute-start.2 = (bf16[160,384]{1,0:T(8,128)(2,1)}, bf16[160,384]{1,0:T(8,128)(2,1)S(1)}, u32[]{:S(2)}, u32[]{:S(2)}) collective-permute-start(bf16[160,384]{1,0:T(8,128)(2,1)} %get-tuple-element.25), channel_id=1, source_target_pairs={{0,3},{1,2},{2,1},{3,0},{4,7},{5,6},{6,5},{7,4},{8,11},{9,10},{10,... | collective-permute-start | bytes 368648 | tf_op jit(solution)/shard_map/ppermute | solution.py:306
  80.7 8.1 %copy-start.1 = (bf16[160,384]{1,0:T(8,128)(2,1)S(1)}, bf16[160,384]{1,0:T(8,128)(2,1)}, u32[]{:S(2)}) copy-start(bf16[160,384]{1,0:T(8,128)(2,1)} %get-tuple-element.22.refs_0_) | copy-start | bytes 368644
  88.8 32.0 %copy-start = (f32[160,64]{0,1:T(8,128)S(1)}, f32[160,64]{0,1:T(8,128)}, u32[]{:S(2)}) copy-start(f32[160,64]{0,1:T(8,128)} %param.14) | copy-start | bytes 122884
  92.8 16.2 %all-to-all-start.1 = ((f32[8,80,128]{2,1,0:T(8,128)}), f32[8,80,128]{2,1,0:T(8,128)S(1)}, u32[]{:S(2)}, u32[]{:S(2)}) async-start(f32[8,80,128]{2,1,0:T(8,128)} %attend_late.1), calls=%async_computation.1 | async-start | bytes 655360 | tf_op jit(solution)/shard_map/all_to_all | solution.py:309

commit v4 on v3

--- a/solution.py
+++ b/solution.py
@@ -300,11 +300,11 @@
     (early,) = pack(*sources, False)
     data = lax.all_to_all(early, "seq", split_axis=0, concat_axis=0, tiled=True)
     late = list(pack(*sources, True))
-    late[3], late[2], data = lax.optimization_barrier((late[3], late[2], data))
+    term, weights = attend_early(data.reshape(groups * rows, data.shape[2]))
+    late[2], late[3], term = lax.optimization_barrier((late[2], late[3], term))
     held = {0: late[0]}
     for e in (1, 4, 5, 6, 7, 2, 3):
         held[e] = lax.ppermute(late[e], "seq", [(i, i ^ e) for i in range(groups)])
-    term, weights = attend_early(data.reshape(groups * rows, data.shape[2]))
     terms = attend_late(place, term, weights, [held[e] for e in range(groups)])
     terms = lax.all_to_all(terms, "seq", split_axis=0, concat_axis=0, tiled=True)
     share = jnp.where(lax.axis_index("cfg") == 0, GUIDANCE, 1.0 - GUIDANCE)

time: 122 us -> 131 us (1.074)
  the two profiles are of different devices: /device:TPU:6 before, /device:TPU:8 now
where the time goes in v4:
time: 131 us
  waiting for transfers between devices  61.6 us (47%)
  starting transfers between devices  38.2 us (29%)
  Pallas kernels  20.7 us (16%)
  blocking collectives  8.59 us (7%)
  between operations  1.44 us (1%)
    all_to_all x1, waiting for transfers between devices, local(): data = lax.all_to_all(early, 'seq', split_axis=0, concat_axis=0, tiled=True)  44.2 us
    ppermute x7, starting transfers between devices, local(): held[e] = lax.ppermute(late[e], 'seq', [(i, i ^ e) for i in range(groups)])  23.6 us
    all_to_all x1, starting transfers between devices, local(): data = lax.all_to_all(early, 'seq', split_axis=0, concat_axis=0, tiled=True)  9.34 us
    all_to_all x1, waiting for transfers between devices, local(): lax.all_to_all(terms, 'seq', split_axis=0, concat_axis=0, tiled=True)  9.07 us
    all_gather x1, blocking collectives, local(): both = lax.all_gather(mine, 'cfg', axis=0)  8.59 us
    pallas_call x2, Pallas kernels, pack(): pl.pallas_call(functools.partial(pack_kernel, groups, late, cuts), out_sh...  8.51 us
    ppermute x7, waiting for transfers between devices, local(): held[e] = lax.ppermute(late[e], 'seq', [(i, i ^ e) for i in range(groups)])  8.27 us
    pallas_call x1, Pallas kernels, attend_early(): pl.pallas_call(functools.partial(early_kernel, chunk), out_shape=[jax.Sha...  7.31 us
  transfers between devices with their start and end apart: 9, of which 4 were waited for; matrix products, arithmetic and copies ran while one was open for 0% of the time, Pallas kernels for 9%

profile of v4, /device:TPU:8, one launch (start us, length us, event | category | flops | bytes accessed | tf_op | source)
XLA Modules:
  0.0 130.6 jit_solution(6901686161845795350)
XLA Ops:
  0.6 4.5 %pack_early.1 = bf16[8,160,896]{2,1,0:T(8,128)(2,1)} custom-call(s32[1]{0:T(128)} %bitcast.place_ref, bf16[160,4096]{1,0:T(8,128)(2,1)} %bitcast.15, bf16[160,4096]{1,0:T(8,128)(2,1)} %bitcast.17, bf16[160,4096]{1,0:T(8,128)(2,1)} %bitcast.19, f32[1,4096]{1,0:T(1,128)} %bitcast.23, f32[1,4096]{1,0:T(1,128)} %bitcast.25, bf16[64,4096]{1,0:T(8,128)(2,1)} %bitcast.21), custom_call_target="tpu_custom_call" | custom-call | flops 268435456 | bytes 8388608 | tf_op jit(solution)/shard_map/pack_early/pallas_call | solution.py:136
  5.1 9.3 %all-to-all-start = ((bf16[8,160,896]{2,1,0:T(8,128)(2,1)}), bf16[8,160,896]{2,1,0:T(8,128)(2,1)S(1)}, u32[]{:S(2)}, u32[]{:S(2)}) async-start(bf16[8,160,896]{2,1,0:T(8,128)(2,1)} %pack_early.1), calls=%async_computation | async-start | bytes 4587520 | tf_op jit(solution)/shard_map/all_to_all | solution.py:301
  14.4 4.1 %pack_late.1 = (bf16[160,384]{1,0:T(8,128)(2,1)}, bf16[160,384]{1,0:T(8,128)(2,1)}, bf16[160,384]{1,0:T(8,128)(2,1)}, bf16[160,384]{1,0:T(8,128)(2,1)}, bf16[160...) custom-call(s32[1]{0:T(128)} %bitcast.place_ref, ...), custom_call_target="tpu_custom_call" | custom-call | flops 268435456 | bytes 8388608 | tf_op jit(solution)/shard_map/pack_late/pallas_call | solution.py:136
  18.5 2.0 %collective-permute-start = (bf16[160,384]{1,0:T(8,128)(2,1)}, bf16[160,384]{1,0:T(8,128)(2,1)S(1)}, u32[]{:S(2)}, u32[]{:S(2)}) collective-permute-start(bf16[160,384]{1,0:T(8,128)(2,1)} %get-tuple-element.23), channel_id=1, source_target_pairs={{0,1},{1,0},{2,3},{3,2},{4,5},{5,4},{6,7},{7,6},{8,9},{9,8},{10,11... | collective-permute-start | bytes 368648 | tf_op jit(solution)/shard_map/ppermute | solution.py:307
  20.5 7.7 %collective-permute-start.3 = (bf16[160,384]{1,0:T(8,128)(2,1)}, bf16[160,384]{1,0:T(8,128)(2,1)S(1)}, u32[]{:S(2)}, u32[]{:S(2)}) collective-permute-start(bf16[160,384]{1,0:T(8,128)(2,1)} %get-tuple-element.26), channel_id=1, source_target_pairs={{0,4},{1,5},{2,6},{3,7},{4,0},{5,1},{6,2},{7,3},{8,12},{9,13},{10,... | collective-permute-start | bytes 368648 | tf_op jit(solution)/shard_map/ppermute | solution.py:307
  28.3 2.4 %collective-permute-start.4 = (bf16[160,384]{1,0:T(8,128)(2,1)}, bf16[160,384]{1,0:T(8,128)(2,1)S(1)}, u32[]{:S(2)}, u32[]{:S(2)}) collective-permute-start(bf16[160,384]{1,0:T(8,128)(2,1)} %get-tuple-element.27), channel_id=1, source_target_pairs={{0,5},{1,4},{2,7},{3,6},{4,1},{5,0},{6,3},{7,2},{8,13},{9,12},{10,... | collective-permute-start | bytes 368648 | tf_op jit(solution)/shard_map/ppermute | solution.py:307
  30.8 4.6 %collective-permute-start.5 = (bf16[160,384]{1,0:T(8,128)(2,1)}, bf16[160,384]{1,0:T(8,128)(2,1)S(1)}, u32[]{:S(2)}, u32[]{:S(2)}) collective-permute-start(bf16[160,384]{1,0:T(8,128)(2,1)} %get-tuple-element.28), channel_id=1, source_target_pairs={{0,6},{1,7},{2,4},{3,5},{4,2},{5,3},{6,0},{7,1},{8,14},{9,15},{10,... | collective-permute-start | bytes 368648 | tf_op jit(solution)/shard_map/ppermute | solution.py:307
  35.4 2.9 %collective-permute-start.6 = (bf16[160,384]{1,0:T(8,128)(2,1)}, bf16[160,384]{1,0:T(8,128)(2,1)S(1)}, u32[]{:S(2)}, u32[]{:S(2)}) collective-permute-start(bf16[160,384]{1,0:T(8,128)(2,1)} %get-tuple-element.29), channel_id=1, source_target_pairs={{0,7},{1,6},{2,5},{3,4},{4,3},{5,2},{6,1},{7,0},{8,15},{9,14},{10,... | collective-permute-start | bytes 368648 | tf_op jit(solution)/shard_map/ppermute | solution.py:307
  38.3 44.2 %all-to-all-done = bf16[8,160,896]{2,1,0:T(8,128)(2,1)S(1)} async-done(((bf16[8,160,896]{2,1,0:T(8,128)(2,1)}), bf16[8,160,896]{2,1,0:T(8,128)(2,1)S(1)}, u32[]{:S(2)}, u32[]{:S(2)}) %all-to-all-start) | async-done | bytes 2293792 | tf_op jit(solution)/shard_map/all_to_all | solution.py:301
  82.5 7.3 %attend_early.1 = (f32[1280,128]{1,0:T(8,128)S(1)}, bf16[1280,1280]{1,0:T(8,128)(2,1)S(1)}) custom-call(bf16[1280,896]{1,0:T(8,128)(2,1)S(1)} %bitcast.12), custom_call_target="tpu_custom_call" | custom-call | flops 8000000000 | bytes 2293760 | tf_op jit(solution)/shard_map/attend_early/pallas_call | solution.py:228
  89.8 0.0 collective-permute-done.refs_1_
  89.8 1.9 %collective-permute-start.1 = (bf16[160,384]{1,0:T(8,128)(2,1)S(1)}, bf16[160,384]{1,0:T(8,128)(2,1)S(1)}, u32[]{:S(2)}, u32[]{:S(2)}) collective-permute-start(bf16[160,384]{1,0:T(8,128)(2,1)S(1)} %copy-done.3), channel_id=1, source_target_pairs={{0,2},{1,3},{2,0},{3,1},{4,6},{5,7},{6,4},{7,5},{8,10},{9,11},{10,... | collective-permute-start | bytes 368648 | tf_op jit(solution)/shard_map/ppermute | solution.py:307
  91.8 0.0 collective-permute-done.3.refs_4_
  91.8 1.9 %collective-permute-start.2 = (bf16[160,384]{1,0:T(8,128)(2,1)S(1)}, bf16[160,384]{1,0:T(8,128)(2,1)S(1)}, u32[]{:S(2)}, u32[]{:S(2)}) collective-permute-start(bf16[160,384]{1,0:T(8,128)(2,1)S(1)} %copy-done.2), channel_id=1, source_target_pairs={{0,3},{1,2},{2,1},{3,0},{4,7},{5,6},{6,5},{7,4},{8,11},{9,10},{10,... | collective-permute-start | bytes 368648 | tf_op jit(solution)/shard_map/ppermute | solution.py:307
  93.7 0.0 collective-permute-done.4.refs_5_
  93.7 0.0 collective-permute-done.5.refs_6_
  93.7 0.0 collective-permute-done.6.refs_7_
  93.8 3.8 %collective-permute-done.1.refs_2_ = bf16[160,384]{1,0:T(8,128)(2,1)S(1)} collective-permute-done((bf16[160,384]{1,0:T(8,128)(2,1)S(1)}, bf16[160,384]{1,0:T(8,128)(2,1)S(1)}, u32[]{:S(2)}, u32[]{:S(2)}) %collective-permute-start.1) | collective-permute-done | bytes 122912 | tf_op jit(solution)/shard_map/ppermute | solution.py:307
  97.5 4.5 %collective-permute-done.2.refs_3_ = bf16[160,384]{1,0:T(8,128)(2,1)S(1)} collective-permute-done((bf16[160,384]{1,0:T(8,128)(2,1)S(1)}, bf16[160,384]{1,0:T(8,128)(2,1)S(1)}, u32[]{:S(2)}, u32[]{:S(2)}) %collective-permute-start.2) | collective-permute-done | bytes 122912 | tf_op jit(solution)/shard_map/ppermute | solution.py:307
  102.0 4.0 %attend_late.1 = f32[8,80,128]{2,1,0:T(8,128)} custom-call(s32[1]{0:T(128)} %bitcast.place_ref, f32[1280,128]{1,0:T(8,128)S(1)} %get-tuple-element.20.term_ref, bf16[1280,1280]{1,0:T(8,128)(2,1)S(1)} %get-tuple-element.21.weights_ref, bf16[160,384]{1,0:T(8,128)(2,1)S(1)} %copy-done.1, bf16[160,384]{1,0:T(8,128)(2,1)S(1)} %collective-permute-done.refs_1_, ...), custom_call_target="tpu_custom_call" | custom-call | flops 3000000000 | bytes 2000000 | tf_op jit(solution)/shard_map/attend_late/pallas_call | solution.py:248
  106.1 5.3 %all-to-all-start.1 = ((f32[8,80,128]{2,1,0:T(8,128)}), f32[8,80,128]{2,1,0:T(8,128)S(1)}, u32[]{:S(2)}, u32[]{:S(2)}) async-start(f32[8,80,128]{2,1,0:T(8,128)} %attend_late.1), calls=%async_computation.1 | async-start | bytes 655360 | tf_op jit(solution)/shard_map/all_to_all | solution.py:309
  112.0 9.1 %all-to-all-done.1 = f32[8,80,128]{2,1,0:T(8,128)S(1)} async-done(((f32[8,80,128]{2,1,0:T(8,128)}), f32[8,80,128]{2,1,0:T(8,128)S(1)}, u32[]{:S(2)}, u32[]{:S(2)}) %all-to-all-start.1) | async-done | bytes 327712 | tf_op jit(solution)/shard_map/all_to_all | solution.py:309
  121.2 8.6 %all-gather = f32[160,128]{1,0:T(8,128)S(1)} all-gather(f32[80,128]{1,0:T(8,128)S(1)} %broadcast_multiply_fusion), channel_id=2, replica_groups=mesh['cfg'=2,'batch'=32,'seq'=8] {'cfg'}, dimensions={0}, use_global_device_ids=true | all-gather | bytes 122880 | tf_op jit(solution)/shard_map/all_gather | solution.py:312
  129.7 0.8 finish.1
  (10 shorter events, 0.0 us)
Async XLA Ops:
  5.1 77.4 %all-to-all-start = ((bf16[8,160,896]{2,1,0:T(8,128)(2,1)}), bf16[8,160,896]{2,1,0:T(8,128)(2,1)S(1)}, u32[]{:S(2)}, u32[]{:S(2)}) async-start(bf16[8,160,896]{2,1,0:T(8,128)(2,1)} %pack_early.1), calls=%async_computation | async-start | bytes 4587520 | tf_op jit(solution)/shard_map/all_to_all | solution.py:301
  18.5 71.3 %collective-permute-start = (bf16[160,384]{1,0:T(8,128)(2,1)}, bf16[160,384]{1,0:T(8,128)(2,1)S(1)}, u32[]{:S(2)}, u32[]{:S(2)}) collective-permute-start(bf16[160,384]{1,0:T(8,128)(2,1)} %get-tuple-element.23), channel_id=1, source_target_pairs={{0,1},{1,0},{2,3},{3,2},{4,5},{5,4},{6,7},{7,6},{8,9},{9,8},{10,11... | collective-permute-start | bytes 368648 | tf_op jit(solution)/shard_map/ppermute | solution.py:307
  20.5 71.2 %collective-permute-start.3 = (bf16[160,384]{1,0:T(8,128)(2,1)}, bf16[160,384]{1,0:T(8,128)(2,1)S(1)}, u32[]{:S(2)}, u32[]{:S(2)}) collective-permute-start(bf16[160,384]{1,0:T(8,128)(2,1)} %get-tuple-element.26), channel_id=1, source_target_pairs={{0,4},{1,5},{2,6},{3,7},{4,0},{5,1},{6,2},{7,3},{8,12},{9,13},{10,... | collective-permute-start | bytes 368648 | tf_op jit(solution)/shard_map/ppermute | solution.py:307
  28.3 65.4 %collective-permute-start.4 = (bf16[160,384]{1,0:T(8,128)(2,1)}, bf16[160,384]{1,0:T(8,128)(2,1)S(1)}, u32[]{:S(2)}, u32[]{:S(2)}) collective-permute-start(bf16[160,384]{1,0:T(8,128)(2,1)} %get-tuple-element.27), channel_id=1, source_target_pairs={{0,5},{1,4},{2,7},{3,6},{4,1},{5,0},{6,3},{7,2},{8,13},{9,12},{10,... | collective-permute-start | bytes 368648 | tf_op jit(solution)/shard_map/ppermute | solution.py:307
  30.8 63.0 %collective-permute-start.5 = (bf16[160,384]{1,0:T(8,128)(2,1)}, bf16[160,384]{1,0:T(8,128)(2,1)S(1)}, u32[]{:S(2)}, u32[]{:S(2)}) collective-permute-start(bf16[160,384]{1,0:T(8,128)(2,1)} %get-tuple-element.28), channel_id=1, source_target_pairs={{0,6},{1,7},{2,4},{3,5},{4,2},{5,3},{6,0},{7,1},{8,14},{9,15},{10,... | collective-permute-start | bytes 368648 | tf_op jit(solution)/shard_map/ppermute | solution.py:307
  35.4 58.4 %collective-permute-start.6 = (bf16[160,384]{1,0:T(8,128)(2,1)}, bf16[160,384]{1,0:T(8,128)(2,1)S(1)}, u32[]{:S(2)}, u32[]{:S(2)}) collective-permute-start(bf16[160,384]{1,0:T(8,128)(2,1)} %get-tuple-element.29), channel_id=1, source_target_pairs={{0,7},{1,6},{2,5},{3,4},{4,3},{5,2},{6,1},{7,0},{8,15},{9,14},{10,... | collective-permute-start | bytes 368648 | tf_op jit(solution)/shard_map/ppermute | solution.py:307
  82.5 7.3 %copy-start.3 = (bf16[160,384]{1,0:T(8,128)(2,1)S(1)}, bf16[160,384]{1,0:T(8,128)(2,1)}, u32[]{:S(2)}) copy-start(bf16[160,384]{1,0:T(8,128)(2,1)} %get-tuple-element.24) | copy-start | bytes 368644
  82.5 9.3 %copy-start.2 = (bf16[160,384]{1,0:T(8,128)(2,1)S(1)}, bf16[160,384]{1,0:T(8,128)(2,1)}, u32[]{:S(2)}) copy-start(bf16[160,384]{1,0:T(8,128)(2,1)} %get-tuple-element.25) | copy-start | bytes 368644
  82.5 19.5 %copy-start.1 = (bf16[160,384]{1,0:T(8,128)(2,1)S(1)}, bf16[160,384]{1,0:T(8,128)(2,1)}, u32[]{:S(2)}) copy-start(bf16[160,384]{1,0:T(8,128)(2,1)} %get-tuple-element.22.refs_0_) | copy-start | bytes 368644
  89.8 7.7 %collective-permute-start.1 = (bf16[160,384]{1,0:T(8,128)(2,1)S(1)}, bf16[160,384]{1,0:T(8,128)(2,1)S(1)}, u32[]{:S(2)}, u32[]{:S(2)}) collective-permute-start(bf16[160,384]{1,0:T(8,128)(2,1)S(1)} %copy-done.3), channel_id=1, source_target_pairs={{0,2},{1,3},{2,0},{3,1},{4,6},{5,7},{6,4},{7,5},{8,10},{9,11},{10,... | collective-permute-start | bytes 368648 | tf_op jit(solution)/shard_map/ppermute | solution.py:307
  91.8 10.2 %collective-permute-start.2 = (bf16[160,384]{1,0:T(8,128)(2,1)S(1)}, bf16[160,384]{1,0:T(8,128)(2,1)S(1)}, u32[]{:S(2)}, u32[]{:S(2)}) collective-permute-start(bf16[160,384]{1,0:T(8,128)(2,1)S(1)} %copy-done.2), channel_id=1, source_target_pairs={{0,3},{1,2},{2,1},{3,0},{4,7},{5,6},{6,5},{7,4},{8,11},{9,10},{10,... | collective-permute-start | bytes 368648 | tf_op jit(solution)/shard_map/ppermute | solution.py:307
  102.0 27.7 %copy-start = (f32[160,64]{0,1:T(8,128)S(1)}, f32[160,64]{0,1:T(8,128)}, u32[]{:S(2)}) copy-start(f32[160,64]{0,1:T(8,128)} %param.14) | copy-start | bytes 122884
  106.1 15.0 %all-to-all-start.1 = ((f32[8,80,128]{2,1,0:T(8,128)}), f32[8,80,128]{2,1,0:T(8,128)S(1)}, u32[]{:S(2)}, u32[]{:S(2)}) async-start(f32[8,80,128]{2,1,0:T(8,128)} %attend_late.1), calls=%async_computation.1 | async-start | bytes 655360 | tf_op jit(solution)/shard_map/all_to_all | solution.py:309

commit v5 on v4

--- a/solution.py
+++ b/solution.py
@@ -170,23 +170,35 @@
     return lax.broadcasted_iota(jnp.int32, (1, 2 * CHANNELS), 1) < CHANNELS
 
 
-def early_kernel(chunk, data_ref, term_ref, weights_ref):
+def early_kernel(chunk, whole, data_ref, out_ref):
     heads = 3
     mapped = data_ref[:, 2 * heads * HEAD_DIM :]
-
-    @pl.loop(0, data_ref.shape[0] // chunk)
-    def _(index):
-        rows = pl.ds(pl.multiple_of(index * chunk, chunk), chunk)
-        terms = []
-        for head in range(heads):
-            lanes = slice(head * HEAD_DIM, (head + 1) * HEAD_DIM)
-            keys = slice((heads + head) * HEAD_DIM, (heads + head + 1) * HEAD_DIM)
-            weights = softmax_weights(scores_between(data_ref[rows, lanes], data_ref[:, keys]))
-            if head < 2:
-                terms.append(jnp.dot(weights, mapped, preferred_element_type=jnp.float32))
-            else:
-                weights_ref[rows, :] = weights
-        term_ref[rows, :] = jnp.where(left_half(), terms[0], terms[1])
+    steps = [
+        (slice(first, first + chunk), head)
+        for first in range(0, data_ref.shape[0], chunk)
+        for head in ((0, 1) if whole else (2,))
+    ]
+
+    def scores_of(rows, head):
+        lanes = slice(head * HEAD_DIM, (head + 1) * HEAD_DIM)
+        keys = slice((heads + head) * HEAD_DIM, (heads + head + 1) * HEAD_DIM)
+        return scores_between(data_ref[rows, lanes], data_ref[:, keys])
+
+    ahead = scores_of(*steps[0])
+    kept = None
+    for index, (rows, head) in enumerate(steps):
+        scores = ahead
+        if index + 1 < len(steps):
+            ahead = scores_of(*steps[index + 1])
+        weights = softmax_weights(scores)
+        if not whole:
+            out_ref[rows, :] = weights
+            continue
+        term = jnp.dot(weights, mapped, preferred_element_type=jnp.float32)
+        if head == 0:
+            kept = term
+        else:
+            out_ref[rows, :] = jnp.where(left_half(), kept, term)
 
 
 def late_kernel(chunk, groups, place_ref, term_ref, weights_ref, *refs):
@@ -222,20 +234,21 @@
             )
 
 
-def attend_early(data, chunk=320):
+def attend_early(data, whole, chunk=320):
     keys = data.shape[0]
     vmem = pl.BlockSpec(memory_space=pltpu.VMEM)
+    if whole:
+        out_shape = jax.ShapeDtypeStruct((keys, 2 * CHANNELS), jnp.float32)
+    else:
+        out_shape = jax.ShapeDtypeStruct((keys, keys), jnp.bfloat16)
     return pl.pallas_call(
-        functools.partial(early_kernel, chunk),
-        out_shape=[
-            jax.ShapeDtypeStruct((keys, 2 * CHANNELS), jnp.float32),
-            jax.ShapeDtypeStruct((keys, keys), jnp.bfloat16),
-        ],
+        functools.partial(early_kernel, chunk, whole),
+        out_shape=out_shape,
         in_specs=[vmem],
-        out_specs=[vmem, vmem],
+        out_specs=vmem,
         compiler_params=params(),
         cost_estimate=pl.CostEstimate(
-            flops=8 * 10**9, bytes_accessed=2 * data.size, transcendentals=3 * keys * keys
+            flops=4 * 10**9, bytes_accessed=2 * data.size, transcendentals=keys * keys
         ),
         name="attend_early",
     )(data)
@@ -300,11 +313,14 @@
     (early,) = pack(*sources, False)
     data = lax.all_to_all(early, "seq", split_axis=0, concat_axis=0, tiled=True)
     late = list(pack(*sources, True))
-    term, weights = attend_early(data.reshape(groups * rows, data.shape[2]))
-    late[2], late[3], term = lax.optimization_barrier((late[2], late[3], term))
+    late[2], data = lax.optimization_barrier((late[2], data))
+    flat = data.reshape(groups * rows, data.shape[2])
+    weights = attend_early(flat, False)
+    late[3], weights, flat = lax.optimization_barrier((late[3], weights, flat))
     held = {0: late[0]}
     for e in (1, 4, 5, 6, 7, 2, 3):
         held[e] = lax.ppermute(late[e], "seq", [(i, i ^ e) for i in range(groups)])
+    term = attend_early(flat, True)
     terms = attend_late(place, term, weights, [held[e] for e in range(groups)])
     terms = lax.all_to_all(terms, "seq", split_axis=0, concat_axis=0, tiled=True)
     share = jnp.where(lax.axis_index("cfg") == 0, GUIDANCE, 1.0 - GUIDANCE)

time: 131 us -> 122 us (0.931)
  the two profiles are of different devices: /device:TPU:8 before, /device:TPU:6 now
where the time goes in v5:
time: 122 us; the launch traced here: 121 us
  waiting for transfers between devices  49.8 us (41%)
  starting transfers between devices  38 us (31%)
  Pallas kernels  20.2 us (17%)
  blocking collectives  11.7 us (10%)
  between operations  1.43 us (1%)
    all_to_all x1, waiting for transfers between devices, local(): data = lax.all_to_all(early, 'seq', split_axis=0, concat_axis=0, tiled=True)  31.3 us
    ppermute x7, starting transfers between devices, local(): held[e] = lax.ppermute(late[e], 'seq', [(i, i ^ e) for i in range(groups)])  26.5 us
    all_to_all x1, waiting for transfers between devices, local(): lax.all_to_all(terms, 'seq', split_axis=0, concat_axis=0, tiled=True)  11.9 us
    all_gather x1, blocking collectives, local(): both = lax.all_gather(mine, 'cfg', axis=0)  11.7 us
    pallas_call x2, Pallas kernels, pack(): pl.pallas_call(functools.partial(pack_kernel, groups, late, cuts), out_sh...  8.51 us
    all_to_all x1, starting transfers between devices, local(): data = lax.all_to_all(early, 'seq', split_axis=0, concat_axis=0, tiled=True)  7.12 us
    pallas_call x2, Pallas kernels, attend_early(): pl.pallas_call(functools.partial(early_kernel, chunk, whole), out_shape=o...  6.78 us
    ppermute x7, waiting for transfers between devices, local(): held[e] = lax.ppermute(late[e], 'seq', [(i, i ^ e) for i in range(groups)])  6.59 us
  transfers between devices with their start and end apart: 9, of which 5 were waited for; matrix products, arithmetic and copies ran while one was open for 0% of the time, Pallas kernels for 9%

profile of v5, /device:TPU:6, one launch (start us, length us, event | category | flops | bytes accessed | tf_op | source)
XLA Modules:
  0.0 121.2 jit_solution(10933251728000500902)
XLA Ops:
  0.6 4.5 %pack_early.1 = bf16[8,160,896]{2,1,0:T(8,128)(2,1)} custom-call(s32[1]{0:T(128)} %bitcast.place_ref, bf16[160,4096]{1,0:T(8,128)(2,1)} %bitcast.16, bf16[160,4096]{1,0:T(8,128)(2,1)} %bitcast.18, bf16[160,4096]{1,0:T(8,128)(2,1)} %bitcast.20, f32[1,4096]{1,0:T(1,128)} %bitcast.24, f32[1,4096]{1,0:T(1,128)} %bitcast.26, bf16[64,4096]{1,0:T(8,128)(2,1)} %bitcast.22), custom_call_target="tpu_custom_call" | custom-call | flops 268435456 | bytes 8388608 | tf_op jit(solution)/shard_map/pack_early/pallas_call | solution.py:136
  5.1 7.1 %all-to-all-start = ((bf16[8,160,896]{2,1,0:T(8,128)(2,1)}), bf16[8,160,896]{2,1,0:T(8,128)(2,1)S(1)}, u32[]{:S(2)}, u32[]{:S(2)}) async-start(bf16[8,160,896]{2,1,0:T(8,128)(2,1)} %pack_early.1), calls=%async_computation | async-start | bytes 4587520 | tf_op jit(solution)/shard_map/all_to_all | solution.py:314
  12.2 4.0 %pack_late.1 = (bf16[160,384]{1,0:T(8,128)(2,1)}, bf16[160,384]{1,0:T(8,128)(2,1)}, bf16[160,384]{1,0:T(8,128)(2,1)}, bf16[160,384]{1,0:T(8,128)(2,1)}, bf16[160...) custom-call(s32[1]{0:T(128)} %bitcast.place_ref, ...), custom_call_target="tpu_custom_call" | custom-call | flops 268435456 | bytes 8388608 | tf_op jit(solution)/shard_map/pack_late/pallas_call | solution.py:136
  16.3 3.9 %collective-permute-start = (bf16[160,384]{1,0:T(8,128)(2,1)}, bf16[160,384]{1,0:T(8,128)(2,1)S(1)}, u32[]{:S(2)}, u32[]{:S(2)}) collective-permute-start(bf16[160,384]{1,0:T(8,128)(2,1)} %get-tuple-element.23), channel_id=1, source_target_pairs={{0,1},{1,0},{2,3},{3,2},{4,5},{5,4},{6,7},{7,6},{8,9},{9,8},{10,11... | collective-permute-start | bytes 368648 | tf_op jit(solution)/shard_map/ppermute | solution.py:322
  20.2 6.4 %collective-permute-start.3 = (bf16[160,384]{1,0:T(8,128)(2,1)}, bf16[160,384]{1,0:T(8,128)(2,1)S(1)}, u32[]{:S(2)}, u32[]{:S(2)}) collective-permute-start(bf16[160,384]{1,0:T(8,128)(2,1)} %get-tuple-element.26), channel_id=1, source_target_pairs={{0,4},{1,5},{2,6},{3,7},{4,0},{5,1},{6,2},{7,3},{8,12},{9,13},{10,... | collective-permute-start | bytes 368648 | tf_op jit(solution)/shard_map/ppermute | solution.py:322
  26.6 1.9 %collective-permute-start.4 = (bf16[160,384]{1,0:T(8,128)(2,1)}, bf16[160,384]{1,0:T(8,128)(2,1)S(1)}, u32[]{:S(2)}, u32[]{:S(2)}) collective-permute-start(bf16[160,384]{1,0:T(8,128)(2,1)} %get-tuple-element.27), channel_id=1, source_target_pairs={{0,5},{1,4},{2,7},{3,6},{4,1},{5,0},{6,3},{7,2},{8,13},{9,12},{10,... | collective-permute-start | bytes 368648 | tf_op jit(solution)/shard_map/ppermute | solution.py:322
  28.5 6.0 %collective-permute-start.5 = (bf16[160,384]{1,0:T(8,128)(2,1)}, bf16[160,384]{1,0:T(8,128)(2,1)S(1)}, u32[]{:S(2)}, u32[]{:S(2)}) collective-permute-start(bf16[160,384]{1,0:T(8,128)(2,1)} %get-tuple-element.28), channel_id=1, source_target_pairs={{0,6},{1,7},{2,4},{3,5},{4,2},{5,3},{6,0},{7,1},{8,14},{9,15},{10,... | collective-permute-start | bytes 368648 | tf_op jit(solution)/shard_map/ppermute | solution.py:322
  34.6 2.5 %collective-permute-start.6 = (bf16[160,384]{1,0:T(8,128)(2,1)}, bf16[160,384]{1,0:T(8,128)(2,1)S(1)}, u32[]{:S(2)}, u32[]{:S(2)}) collective-permute-start(bf16[160,384]{1,0:T(8,128)(2,1)} %get-tuple-element.29), channel_id=1, source_target_pairs={{0,7},{1,6},{2,5},{3,4},{4,3},{5,2},{6,1},{7,0},{8,15},{9,14},{10,... | collective-permute-start | bytes 368648 | tf_op jit(solution)/shard_map/ppermute | solution.py:322
  37.0 31.3 %all-to-all-done = bf16[8,160,896]{2,1,0:T(8,128)(2,1)S(1)} async-done(((bf16[8,160,896]{2,1,0:T(8,128)(2,1)}), bf16[8,160,896]{2,1,0:T(8,128)(2,1)S(1)}, u32[]{:S(2)}, u32[]{:S(2)}) %all-to-all-start) | async-done | bytes 2293792 | tf_op jit(solution)/shard_map/all_to_all | solution.py:314
  68.3 2.0 %attend_early.2.weights_ref = bf16[1280,1280]{1,0:T(8,128)(2,1)S(1)} custom-call(bf16[1280,896]{1,0:T(8,128)(2,1)S(1)} %bitcast.12), custom_call_target="tpu_custom_call" | custom-call | flops 4000000000 | bytes 2293760 | tf_op jit(solution)/shard_map/attend_early/pallas_call | solution.py:244
  70.3 2.8 %collective-permute-done.refs_1_ = bf16[160,384]{1,0:T(8,128)(2,1)S(1)} collective-permute-done((bf16[160,384]{1,0:T(8,128)(2,1)}, bf16[160,384]{1,0:T(8,128)(2,1)S(1)}, u32[]{:S(2)}, u32[]{:S(2)}) %collective-permute-start) | collective-permute-done | bytes 122912 | tf_op jit(solution)/shard_map/ppermute | solution.py:322
  73.1 1.9 %collective-permute-start.2 = (bf16[160,384]{1,0:T(8,128)(2,1)S(1)}, bf16[160,384]{1,0:T(8,128)(2,1)S(1)}, u32[]{:S(2)}, u32[]{:S(2)}) collective-permute-start(bf16[160,384]{1,0:T(8,128)(2,1)S(1)} %copy-done.3), channel_id=1, source_target_pairs={{0,3},{1,2},{2,1},{3,0},{4,7},{5,6},{6,5},{7,4},{8,11},{9,10},{10,... | collective-permute-start | bytes 368648 | tf_op jit(solution)/shard_map/ppermute | solution.py:322
  75.0 3.1 %collective-permute-done.3.refs_4_ = bf16[160,384]{1,0:T(8,128)(2,1)S(1)} collective-permute-done((bf16[160,384]{1,0:T(8,128)(2,1)}, bf16[160,384]{1,0:T(8,128)(2,1)S(1)}, u32[]{:S(2)}, u32[]{:S(2)}) %collective-permute-start.3) | collective-permute-done | bytes 122912 | tf_op jit(solution)/shard_map/ppermute | solution.py:322
  78.1 3.8 %collective-permute-start.1 = (bf16[160,384]{1,0:T(8,128)(2,1)S(1)}, bf16[160,384]{1,0:T(8,128)(2,1)S(1)}, u32[]{:S(2)}, u32[]{:S(2)}) collective-permute-start(bf16[160,384]{1,0:T(8,128)(2,1)S(1)} %copy-done.2), channel_id=1, source_target_pairs={{0,2},{1,3},{2,0},{3,1},{4,6},{5,7},{6,4},{7,5},{8,10},{9,11},{10,... | collective-permute-start | bytes 368648 | tf_op jit(solution)/shard_map/ppermute | solution.py:322
  82.0 4.8 %attend_early.3.term_ref = f32[1280,128]{1,0:T(8,128)S(1)} custom-call(bf16[1280,896]{1,0:T(8,128)(2,1)S(1)} %bitcast.13), custom_call_target="tpu_custom_call" | custom-call | flops 4000000000 | bytes 2293760 | tf_op jit(solution)/shard_map/attend_early/pallas_call | solution.py:244
  86.8 0.0 collective-permute-done.4.refs_5_
  86.8 0.0 collective-permute-done.5.refs_6_
  86.8 0.0 collective-permute-done.6.refs_7_
  86.8 0.7 collective-permute-done.1.refs_2_
  87.5 4.1 %attend_late.1 = f32[8,80,128]{2,1,0:T(8,128)} custom-call(s32[1]{0:T(128)} %bitcast.place_ref, f32[1280,128]{1,0:T(8,128)S(1)} %attend_early.3.term_ref, bf16[1280,1280]{1,0:T(8,128)(2,1)S(1)} %attend_early.2.weights_ref, bf16[160,384]{1,0:T(8,128)(2,1)S(1)} %copy-done.1, bf16[160,384]{1,0:T(8,128)(2,1)S(1)} %collective-permute-done.refs_1_, ...), custom_call_target="tpu_custom_call" | custom-call | flops 3000000000 | bytes 2000000 | tf_op jit(solution)/shard_map/attend_late/pallas_call | solution.py:261
  91.6 4.5 %all-to-all-start.1 = ((f32[8,80,128]{2,1,0:T(8,128)}), f32[8,80,128]{2,1,0:T(8,128)S(1)}, u32[]{:S(2)}, u32[]{:S(2)}) async-start(f32[8,80,128]{2,1,0:T(8,128)} %attend_late.1), calls=%async_computation.1 | async-start | bytes 655360 | tf_op jit(solution)/shard_map/all_to_all | solution.py:325
  96.7 11.9 %all-to-all-done.1 = f32[8,80,128]{2,1,0:T(8,128)S(1)} async-done(((f32[8,80,128]{2,1,0:T(8,128)}), f32[8,80,128]{2,1,0:T(8,128)S(1)}, u32[]{:S(2)}, u32[]{:S(2)}) %all-to-all-start.1) | async-done | bytes 327712 | tf_op jit(solution)/shard_map/all_to_all | solution.py:325
  108.7 11.7 %all-gather = f32[160,128]{1,0:T(8,128)S(1)} all-gather(f32[80,128]{1,0:T(8,128)S(1)} %broadcast_multiply_fusion), channel_id=2, replica_groups=mesh['cfg'=2,'batch'=32,'seq'=8] {'cfg'}, dimensions={0}, use_global_device_ids=true | all-gather | bytes 122880 | tf_op jit(solution)/shard_map/all_gather | solution.py:328
  120.4 0.8 finish.1
  (11 shorter events, 0.0 us)
Async XLA Ops:
  5.1 63.2 %all-to-all-start = ((bf16[8,160,896]{2,1,0:T(8,128)(2,1)}), bf16[8,160,896]{2,1,0:T(8,128)(2,1)S(1)}, u32[]{:S(2)}, u32[]{:S(2)}) async-start(bf16[8,160,896]{2,1,0:T(8,128)(2,1)} %pack_early.1), calls=%async_computation | async-start | bytes 4587520 | tf_op jit(solution)/shard_map/all_to_all | solution.py:314
  16.3 56.8 %collective-permute-start = (bf16[160,384]{1,0:T(8,128)(2,1)}, bf16[160,384]{1,0:T(8,128)(2,1)S(1)}, u32[]{:S(2)}, u32[]{:S(2)}) collective-permute-start(bf16[160,384]{1,0:T(8,128)(2,1)} %get-tuple-element.23), channel_id=1, source_target_pairs={{0,1},{1,0},{2,3},{3,2},{4,5},{5,4},{6,7},{7,6},{8,9},{9,8},{10,11... | collective-permute-start | bytes 368648 | tf_op jit(solution)/shard_map/ppermute | solution.py:322
  20.2 57.9 %collective-permute-start.3 = (bf16[160,384]{1,0:T(8,128)(2,1)}, bf16[160,384]{1,0:T(8,128)(2,1)S(1)}, u32[]{:S(2)}, u32[]{:S(2)}) collective-permute-start(bf16[160,384]{1,0:T(8,128)(2,1)} %get-tuple-element.26), channel_id=1, source_target_pairs={{0,4},{1,5},{2,6},{3,7},{4,0},{5,1},{6,2},{7,3},{8,12},{9,13},{10,... | collective-permute-start | bytes 368648 | tf_op jit(solution)/shard_map/ppermute | solution.py:322
  26.6 60.2 %collective-permute-start.4 = (bf16[160,384]{1,0:T(8,128)(2,1)}, bf16[160,384]{1,0:T(8,128)(2,1)S(1)}, u32[]{:S(2)}, u32[]{:S(2)}) collective-permute-start(bf16[160,384]{1,0:T(8,128)(2,1)} %get-tuple-element.27), channel_id=1, source_target_pairs={{0,5},{1,4},{2,7},{3,6},{4,1},{5,0},{6,3},{7,2},{8,13},{9,12},{10,... | collective-permute-start | bytes 368648 | tf_op jit(solution)/shard_map/ppermute | solution.py:322
  28.5 58.2 %collective-permute-start.5 = (bf16[160,384]{1,0:T(8,128)(2,1)}, bf16[160,384]{1,0:T(8,128)(2,1)S(1)}, u32[]{:S(2)}, u32[]{:S(2)}) collective-permute-start(bf16[160,384]{1,0:T(8,128)(2,1)} %get-tuple-element.28), channel_id=1, source_target_pairs={{0,6},{1,7},{2,4},{3,5},{4,2},{5,3},{6,0},{7,1},{8,14},{9,15},{10,... | collective-permute-start | bytes 368648 | tf_op jit(solution)/shard_map/ppermute | solution.py:322
  34.6 52.2 %collective-permute-start.6 = (bf16[160,384]{1,0:T(8,128)(2,1)}, bf16[160,384]{1,0:T(8,128)(2,1)S(1)}, u32[]{:S(2)}, u32[]{:S(2)}) collective-permute-start(bf16[160,384]{1,0:T(8,128)(2,1)} %get-tuple-element.29), channel_id=1, source_target_pairs={{0,7},{1,6},{2,5},{3,4},{4,3},{5,2},{6,1},{7,0},{8,15},{9,14},{10,... | collective-permute-start | bytes 368648 | tf_op jit(solution)/shard_map/ppermute | solution.py:322
  68.3 4.8 %copy-start.3 = (bf16[160,384]{1,0:T(8,128)(2,1)S(1)}, bf16[160,384]{1,0:T(8,128)(2,1)}, u32[]{:S(2)}) copy-start(bf16[160,384]{1,0:T(8,128)(2,1)} %get-tuple-element.25) | copy-start | bytes 368644
  68.3 9.8 %copy-start.2 = (bf16[160,384]{1,0:T(8,128)(2,1)S(1)}, bf16[160,384]{1,0:T(8,128)(2,1)}, u32[]{:S(2)}) copy-start(bf16[160,384]{1,0:T(8,128)(2,1)} %get-tuple-element.24) | copy-start | bytes 368644
  70.3 17.2 %copy-start.1 = (bf16[160,384]{1,0:T(8,128)(2,1)S(1)}, bf16[160,384]{1,0:T(8,128)(2,1)}, u32[]{:S(2)}) copy-start(bf16[160,384]{1,0:T(8,128)(2,1)} %get-tuple-element.22.refs_0_) | copy-start | bytes 368644
  73.1 13.7 %collective-permute-start.2 = (bf16[160,384]{1,0:T(8,128)(2,1)S(1)}, bf16[160,384]{1,0:T(8,128)(2,1)S(1)}, u32[]{:S(2)}, u32[]{:S(2)}) collective-permute-start(bf16[160,384]{1,0:T(8,128)(2,1)S(1)} %copy-done.3), channel_id=1, source_target_pairs={{0,3},{1,2},{2,1},{3,0},{4,7},{5,6},{6,5},{7,4},{8,11},{9,10},{10,... | collective-permute-start | bytes 368648 | tf_op jit(solution)/shard_map/ppermute | solution.py:322
  78.1 9.4 %collective-permute-start.1 = (bf16[160,384]{1,0:T(8,128)(2,1)S(1)}, bf16[160,384]{1,0:T(8,128)(2,1)S(1)}, u32[]{:S(2)}, u32[]{:S(2)}) collective-permute-start(bf16[160,384]{1,0:T(8,128)(2,1)S(1)} %copy-done.2), channel_id=1, source_target_pairs={{0,2},{1,3},{2,0},{3,1},{4,6},{5,7},{6,4},{7,5},{8,10},{9,11},{10,... | collective-permute-start | bytes 368648 | tf_op jit(solution)/shard_map/ppermute | solution.py:322
  87.5 32.8 %copy-start = (f32[160,64]{0,1:T(8,128)S(1)}, f32[160,64]{0,1:T(8,128)}, u32[]{:S(2)}) copy-start(f32[160,64]{0,1:T(8,128)} %param.14) | copy-start | bytes 122884
  91.6 17.0 %all-to-all-start.1 = ((f32[8,80,128]{2,1,0:T(8,128)}), f32[8,80,128]{2,1,0:T(8,128)S(1)}, u32[]{:S(2)}, u32[]{:S(2)}) async-start(f32[8,80,128]{2,1,0:T(8,128)} %attend_late.1), calls=%async_computation.1 | async-start | bytes 655360 | tf_op jit(solution)/shard_map/all_to_all | solution.py:325
